TPU v7x, 256 devices: a whole 4x4x8 slice. The times are simulated.
256 devices in a mesh: ep: 64 (over y_hi, z, x), ctr: 4 (over y_lo, core).
Axes of the slice: x: 4, y: 4 (y_hi: 2, y_lo: 2; y = y_hi * 2 + y_lo), z: 8, core: 2. Of those that a mesh axis runs over, the one named last changes fastest.
Arguments:
- episodes: bfloat16 [96, 32768], P(None, 'ep'), may hold values from -10 to 10
- centers: bfloat16 [96, 65536], P(None, 'ctr'), may hold values from -10 to 10
- coeffs: float32 [32, 65536], P(None, ('ctr', 'ep')), may hold values from -6 to 6
- residual: float32 [32, 65536], P(None, ('ctr', 'ep')), may hold values from -6 to 6
- direction: float32 [32, 65536], P(None, ('ctr', 'ep')), may hold values from -6 to 6
Outputs:
- coeffs_next: float32 [32, 65536], P(None, ('ctr', 'ep'))
- residual_next: float32 [32, 65536], P(None, ('ctr', 'ep'))
- direction_next: float32 [32, 65536], P(None, ('ctr', 'ep'))
All inputs are finite; a program needn't handle non-finite values.
Results may differ from a plain program's by a relative error of at most 0.00076.
Values may be sent and summed in bfloat16 or wider, within the bound.
No kernel may reach another device: no remote copies, remote signals or barrier semaphores. Data moves between devices by JAX's collectives and lax.ppermute only.
A program may use at most 64 MiB of HBM per device.

v0:
```python
import math

import jax
import jax.numpy as jnp
from jax import lax
from jax.sharding import PartitionSpec as P


def kernel_tile(left_feat, left_norms, right_feat, right_norms, sharpness):
    cross = lax.dot_general(
        left_feat, right_feat, (((0,), (0,)), ((), ())), preferred_element_type=jnp.float32
    )
    distance = left_norms[:, None] + right_norms[None, :] - 2.0 * cross
    return jnp.exp(-sharpness * distance).astype(jnp.bfloat16)


def shards(episodes, centers, coeffs, residual, direction):
    features = episodes.shape[0]
    sharpness = 3.0 / features
    row_count = episodes.shape[1]
    targets = direction.shape[0]
    ep_norms = jnp.sum(jnp.square(episodes.astype(jnp.float32)), axis=0)
    cen_norms = jnp.sum(jnp.square(centers.astype(jnp.float32)), axis=0)
    old_norm = lax.psum(jnp.sum(residual * residual, axis=1), ("ep", "ctr"))
    dir_half = direction.astype(jnp.bfloat16)
    piece = lax.all_gather(dir_half, "ep", axis=1, tiled=True)
    piece_cols = piece.shape[1]
    forward_block = math.gcd(piece_cols, 2048)

    def advance(block_idx, running):
        offset = block_idx * forward_block
        cols = lax.dynamic_slice_in_dim(centers, offset, forward_block, 1)
        col_norms = lax.dynamic_slice_in_dim(cen_norms, offset, forward_block, 0)
        kernel = kernel_tile(episodes, ep_norms, cols, col_norms, sharpness)
        column_part = lax.dynamic_slice_in_dim(piece, offset, forward_block, 1)
        return running + lax.dot_general(
            column_part, kernel, (((1,), (1,)), ((), ())), preferred_element_type=jnp.float32
        )

    partial_value = lax.fori_loop(
        0, piece_cols // forward_block, advance, jnp.zeros((targets, row_count), jnp.float32)
    )
    row_half = lax.psum(partial_value, "ctr").astype(jnp.bfloat16)
    local_cols = centers.shape[1]
    block = math.gcd(local_cols, 2048)

    def project(block_idx, running):
        offset = block_idx * block
        cols = lax.dynamic_slice_in_dim(centers, offset, block, 1)
        col_norms = lax.dynamic_slice_in_dim(cen_norms, offset, block, 0)
        kernel = kernel_tile(episodes, ep_norms, cols, col_norms, sharpness)
        return lax.dynamic_update_slice_in_dim(
            running, jnp.dot(row_half, kernel, preferred_element_type=jnp.float32), offset, 1
        )

    col_terms = lax.fori_loop(
        0, local_cols // block, project, jnp.zeros((targets, local_cols), jnp.float32)
    )
    gram_cols = lax.psum_scatter(col_terms, "ep", scatter_dimension=1, tiled=True)
    applied = gram_cols + 1.0 * direction
    curvature = lax.psum(jnp.sum(direction * applied, axis=1), ("ep", "ctr"))
    step_size = old_norm / curvature
    residual_next = residual - step_size[:, None] * applied
    new_norm = lax.psum(jnp.sum(residual_next * residual_next, axis=1), ("ep", "ctr"))
    coeffs_next = coeffs + step_size[:, None] * direction
    direction_next = residual_next + (new_norm / old_norm)[:, None] * direction
    return (coeffs_next, residual_next, direction_next)


def solution(mesh):
    placed = (
        P(None, "ep"),
        P(None, "ctr"),
        P(None, ("ctr", "ep")),
        P(None, ("ctr", "ep")),
        P(None, ("ctr", "ep")),
    )
    return jax.shard_map(
        shards,
        mesh=mesh,
        in_specs=placed,
        out_specs=(P(None, ("ctr", "ep")), P(None, ("ctr", "ep")), P(None, ("ctr", "ep"))),
        check_vma=False,
    )
```

profile of v0, /device:TPU:1, one launch (start us, length us, event | category | flops | bytes accessed | tf_op | source)
XLA Modules:
  0.0 691.3 jit_solution(14260735397435764624)
XLA Ops:
  9.6 2.6 multiply_reduce_fusion
  12.2 104.7 %all-gather.2.cloned.1.call-done = bf16[32,16384]{1,0:T(8,128)(2,1)} async-done(((bf16[32,256]{1,0:T(8,128)(2,1)}), bf16[32,16384]{1,0:T(8,128)(2,1)}) %all-gather.2.cloned.1.call-update) | async-done | bytes 1048592 | tf_op jit(solution)/shard_map/all_gather | solution.py:26
  116.9 21.5 %while.28 = (s32[]{:T(128)}, f32[32,512]{1,0:T(8,128)S(1)}, bf16[32,16384]{1,0:T(8,128)(2,1)}, f32[512]{0:T(512)S(1)}, f32[16384]{0:T(1024)S(1)}, /*index=5*/bf1...) while((s32[]{:T(128)}, f32[32,512]{1,0:T(8,128)S(1)}, ...), condition=%wide.region_5.0_spmd.clone, body=%wide.region_4.0_spmd.clone.sunk | while | flops 273711104 | bytes 781992 | solution.py:40
  116.9 2.6 fusion.40
  119.6 2.6 fusion.40
  122.3 2.6 fusion.40
  125.0 2.6 fusion.40
  127.7 2.6 fusion.40
  130.4 2.6 fusion.40
  133.1 2.6 fusion.40
  135.8 2.6 fusion.40
  138.4 13.7 %psum.29 = bf16[32,512]{1,0:T(8,128)(2,1)S(1)} all-reduce(f32[32,512]{1,0:T(8,128)S(1)} %get-tuple-element.251), channel_id=1, replica_groups=mesh['ep'=64,'ctr'=4] {'ctr'}, use_global_device_ids=true, to_apply=%region_6.0 | all-reduce | flops 16384 | bytes 98304 | tf_op jit(solution)/shard_map/psum | solution.py:43
  152.4 19.1 %while.27 = (s32[]{:T(128)}, f32[32,16384]{1,0:T(8,128)S(1)}, f32[512]{0:T(512)S(1)}, f32[16384]{0:T(1024)S(1)}, bf16[96,16384]{1,0:T(8,128)(2,1)}, /*index=5*/b...) while((s32[]{:T(128)}, f32[32,16384]{1,0:T(8,128)S(1)}, ...), condition=%wide.region_8.0_spmd, body=%wide.region_7.0_spmd.sunk | while | flops 273678336 | bytes 814239 | solution.py:56
  152.4 2.4 fusion.36
  154.8 2.4 fusion.36
  157.2 2.4 fusion.36
  159.5 2.4 fusion.36
  161.9 2.4 fusion.36
  164.3 2.4 fusion.36
  166.7 2.4 fusion.36
  169.1 2.4 fusion.36
  173.0 311.1 %reduce-scatter.2.cloned.1.call-done = f32[32,256]{1,0:T(8,128)} async-done(((f32[32,16384]{1,0:T(8,128)}), f32[32,256]{1,0:T(8,128)}) %reduce-scatter.2.cloned.1.call-update) | async-done | bytes 32784 | tf_op jit(solution)/shard_map/reduce_scatter | solution.py:59
  484.9 124.5 %all-reduce = (f32[32]{0:T(128)S(1)}, f32[32]{0:T(128)S(1)}) all-reduce(f32[32]{0:T(128)S(1)} %multiply_reduce_fusion.4, f32[32]{0:T(128)S(1)} %get-tuple-element.309), channel_id=1, replica_groups=mesh['ep'=64,'ctr'=4] {'ep','ctr'}, use_global_device_ids=true, to_apply=%region_1.0 | all-reduce | flops 64 | bytes 512 | tf_op jit(solution)/shard_map/psum | solution.py:24
  609.7 74.1 %psum.31 = f32[32]{0:T(128)S(1)} all-reduce(f32[32]{0:T(128)S(1)} %get-tuple-element.307), channel_id=1, replica_groups=mesh['ep'=64,'ctr'=4] {'ep','ctr'}, use_global_device_ids=true, to_apply=%region_13.0 | all-reduce | flops 32 | bytes 256 | tf_op jit(solution)/shard_map/psum | solution.py:64
  (42 shorter events, 5.9 us)
Async XLA Ops:
  7.2 109.8 %copy-start.4 = (bf16[96,512]{1,0:T(8,128)(2,1)S(1)}, bf16[96,512]{1,0:T(8,128)(2,1)}, u32[]{:S(2)}) copy-start(bf16[96,512]{1,0:T(8,128)(2,1)} %param.9) | copy-start | bytes 294916
  7.2 109.7 %all-gather.2.cloned.1.call-start = ((), (), s32[]{:S(2)}) async-start(), calls=%async_computation.1 | async-start | bytes 1064960 | tf_op jit(solution)/shard_map/all_gather | solution.py:26
  8.6 475.4 %reduce-scatter.2.cloned.1.call-start = ((), (), s32[]{:S(2)}) async-start(), calls=%async_computation.2 | async-start | bytes 2129920 | tf_op jit(solution)/shard_map/reduce_scatter | solution.py:59
  152.3 20.6 %copy-start.3 = (f32[32,256]{1,0:T(8,128)S(1)}, f32[32,256]{1,0:T(8,128)}, u32[]{:S(2)}) copy-start(f32[32,256]{1,0:T(8,128)} %param.12) | copy-start | bytes 98308
  152.3 331.7 %copy-start.1 = (f32[32,256]{1,0:T(8,128)S(1)}, f32[32,256]{1,0:T(8,128)}, u32[]{:S(2)}) copy-start(f32[32,256]{1,0:T(8,128)} %param.13) | copy-start | bytes 98308
  152.3 531.5 %copy-start.5 = (f32[32,256]{1,0:T(8,128)S(1)}, f32[32,256]{1,0:T(8,128)}, u32[]{:S(2)}) copy-start(f32[32,256]{1,0:T(8,128)} %param.11) | copy-start | bytes 98308
  171.5 1.4 copy-start
  609.7 74.8 %copy-start.2 = (f32[32,256]{1,0:T(8,128)}, f32[32,256]{1,0:T(8,128)S(1)}, u32[]{:S(2)}) copy-start(f32[32,256]{1,0:T(8,128)S(1)} %get-tuple-element.308) | copy-start | bytes 98308
Sparse Core Ops, SparseCore 0:
  12.0 104.8 all-gather.1
  173.0 311.0 reduce-scatter.1
where the time goes:
time: 692 us; the launch traced here: 691 us
  waiting for transfers between devices  416 us (60%)
  blocking collectives  212 us (31%)
  matrix products  40.2 us (6%)
  between operations  14.1 us (2%)
    reduce_scatter x1, waiting for transfers between devices, shards(): lax.psum_scatter(col_terms, 'ep', scatter_dimension=1, tiled=True)  311 us
    psum x1, blocking collectives, shards(): old_norm = lax.psum(jnp.sum(residual * residual, axis=1), ('ep', 'ctr'))  125 us
    all_gather x1, waiting for transfers between devices, shards(): piece = lax.all_gather(dir_half, 'ep', axis=1, tiled=True)  105 us
    psum x1, blocking collectives, shards(): lax.psum(jnp.sum(residual_next * residual_next, axis=1), ('ep', 'ctr'))  74.1 us
    dot_general x8, matrix products, advance(): lax.dot_general(column_part, kernel, (((1,), (1,)), ((), ())), preferred_...  21.2 us
    dot_general x8, matrix products, project(): jnp.dot(row_half, kernel, preferred_element_type=jnp.float32)  19.1 us
  transfers between devices with their start and end apart: 2, of which 2 were waited for; matrix products, arithmetic and copies ran while one was open for 1% of the time, Pallas kernels for 0%

commit v1 on v0

v1 whole, which is shorter than its diff:
```python
import jax
import jax.numpy as jnp
from jax import lax
from jax.experimental import pallas as pl
from jax.experimental.pallas import tpu as pltpu
from jax.sharding import Mesh, PartitionSpec as P

AXES = ("yh", "z", "x", "yl", "c")
SIZES = (2, 8, 4, 2, 2)
SIZE = dict(zip(AXES, SIZES))
EP = ("yh", "z", "x")
CTR = ("yl", "c")
SPLIT = ("yh", "z")
MERGED = tuple(a for a in EP if a not in SPLIT)
ROWS = MERGED + CTR

F = 96
DEPTH = 128
TGT = 32
PIECE = 256
ROWPIECE = 128
SHARP = 3.0 / F
F32 = jnp.float32
BF16 = jnp.bfloat16
VMEM = 48 * 1024 * 1024


def prod(axes):
    out = 1
    for a in axes:
        out *= SIZE[a]
    return out


N_SPLIT, N_MERGED, N_ROWS = prod(SPLIT), prod(MERGED), prod(ROWS)
N_EP = 512 * N_MERGED


def three(v):
    hi = v.astype(BF16).astype(F32)
    mid = (v - hi).astype(BF16).astype(F32)
    return hi, mid, v - hi - mid


def extra_rows(norm_parts, first, width):
    row = lax.broadcasted_iota(jnp.int32, (DEPTH - F, width), 0)
    out = jnp.where(row < 6, 1.0, 0.0).astype(F32)
    for k, part in enumerate(norm_parts):
        out = jnp.where(row == first + k, part, out)
    return out


def tile_kernel(blocks, eps_ref, cen_ref, out_ref, left):
    @pl.when(pl.program_id(0) == 0)
    def _():
        for m in range(N_MERGED):
            e = eps_ref[m].astype(F32)
            norm = jnp.sum(e * e, axis=0, keepdims=True)
            tall = jnp.concatenate([e * (2.0 * SHARP), extra_rows(three(-SHARP * norm), 0, 512)], axis=0)
            left[m * 512:(m + 1) * 512, :] = tall.T.astype(BF16)

    c = cen_ref[...].astype(F32)
    norm = jnp.sum(c * c, axis=0, keepdims=True)
    right = jnp.concatenate([cen_ref[...], extra_rows(three(-SHARP * norm), 3, PIECE).astype(BF16)], axis=0)
    for r in range(0, N_EP, 256):
        arg = jnp.dot(left[r:r + 256, :], right, preferred_element_type=F32)
        out_ref[0, r:r + 256, :] = jnp.exp(arg).astype(BF16)


def tiles(blocks, eps, centers):
    return pl.pallas_call(
        tile_kernel,
        grid_spec=pltpu.PrefetchScalarGridSpec(
            num_scalar_prefetch=1,
            grid=(N_SPLIT,),
            in_specs=[
                pl.BlockSpec((N_MERGED, F, 512), lambda i, b: (0, 0, 0)),
                pl.BlockSpec((F, PIECE), lambda i, b: (0, b[i])),
            ],
            out_specs=pl.BlockSpec((1, N_EP, PIECE), lambda i, b: (i, 0, 0)),
            scratch_shapes=[pltpu.VMEM((N_EP, DEPTH), BF16)],
        ),
        out_shape=jax.ShapeDtypeStruct((N_SPLIT, N_EP, PIECE), BF16),
        compiler_params=pltpu.CompilerParams(vmem_limit_bytes=VMEM),
        cost_estimate=pl.CostEstimate(
            flops=2 * DEPTH * 2 ** 23, bytes_accessed=2 ** 24, transcendentals=2 ** 23
        ),
    )(blocks, eps, centers)


def row_kernel(d_ref, k_ref, out_ref, total):
    i = pl.program_id(0)

    @pl.when(i == 0)
    def _():
        total[...] = jnp.zeros_like(total)

    total[...] += lax.dot_general(d_ref[0], k_ref[0], (((1,), (1,)), ((), ())), preferred_element_type=F32)

    @pl.when(i == N_SPLIT - 1)
    def _():
        for j in range(N_ROWS):
            out_ref[j] = total[:, j * ROWPIECE:(j + 1) * ROWPIECE]


def row_sums(dirs, kmat):
    return pl.pallas_call(
        row_kernel,
        grid=(N_SPLIT,),
        in_specs=[
            pl.BlockSpec((1, TGT, PIECE), lambda i: (i, 0, 0)),
            pl.BlockSpec((1, N_EP, PIECE), lambda i: (i, 0, 0)),
        ],
        out_specs=pl.BlockSpec((N_ROWS, TGT, ROWPIECE), lambda i: (0, 0, 0)),
        out_shape=jax.ShapeDtypeStruct((N_ROWS, TGT, ROWPIECE), F32),
        scratch_shapes=[pltpu.VMEM((TGT, N_EP), F32)],
        compiler_params=pltpu.CompilerParams(vmem_limit_bytes=VMEM),
        cost_estimate=pl.CostEstimate(flops=2 * TGT * 2 ** 23, bytes_accessed=2 ** 24, transcendentals=0),
    )(dirs, kmat)


def spread_kernel(parts_ref, out_ref):
    half = jnp.sum(parts_ref[...], axis=0).astype(BF16)
    for j in range(N_ROWS):
        out_ref[j] = half


def spread(parts):
    return pl.pallas_call(
        spread_kernel, out_shape=jax.ShapeDtypeStruct((N_ROWS, TGT, ROWPIECE), BF16)
    )(parts)


def column_kernel(rows_ref, k_ref, out_ref, half):
    @pl.when(pl.program_id(0) == 0)
    def _():
        for j in range(N_ROWS):
            half[:, j * ROWPIECE:(j + 1) * ROWPIECE] = rows_ref[j]

    out_ref[0] = jnp.dot(half[...], k_ref[0], preferred_element_type=F32)


def column_sums(rows, kmat):
    return pl.pallas_call(
        column_kernel,
        grid=(N_SPLIT,),
        in_specs=[
            pl.BlockSpec((N_ROWS, TGT, ROWPIECE), lambda i: (0, 0, 0)),
            pl.BlockSpec((1, N_EP, PIECE), lambda i: (i, 0, 0)),
        ],
        out_specs=pl.BlockSpec((1, TGT, PIECE), lambda i: (i, 0, 0)),
        out_shape=jax.ShapeDtypeStruct((N_SPLIT, TGT, PIECE), F32),
        scratch_shapes=[pltpu.VMEM((TGT, N_EP), BF16)],
        compiler_params=pltpu.CompilerParams(vmem_limit_bytes=VMEM),
        cost_estimate=pl.CostEstimate(flops=2 * TGT * 2 ** 23, bytes_accessed=2 ** 24, transcendentals=0),
    )(rows, kmat)


def apply_kernel(parts_ref, r_ref, d_ref, applied_ref, sums_ref):
    r, d = r_ref[...], d_ref[...]
    a = jnp.sum(parts_ref[...], axis=0) + 1.0 * d
    applied_ref[...] = a
    terms = [p[:, :128] + p[:, 128:] for p in (r * r, r * a, d * a, a * a)]
    line = jnp.sum(jnp.concatenate(terms, axis=0).T, axis=0, keepdims=True)
    sums_ref[...] = jnp.broadcast_to(line, sums_ref.shape)


def apply_and_sum(parts, residual, direction):
    return pl.pallas_call(
        apply_kernel,
        out_shape=(
            jax.ShapeDtypeStruct((TGT, PIECE), F32),
            jax.ShapeDtypeStruct((256, 4 * TGT), F32),
        ),
    )(parts, residual, direction)


def step_kernel(sums_ref, coeffs_ref, r_ref, d_ref, a_ref, co_ref, ro_ref, do_ref, step_ref, doubt_ref):
    total = jnp.sum(sums_ref[...], axis=0, keepdims=True)
    cols = jnp.broadcast_to(total, (128, 128)).T
    old, ra, curv, aa = (cols[k * TGT:(k + 1) * TGT] for k in range(4))
    step = old / curv
    grown = step * (step * aa)
    new = old - 2.0 * (step * ra) + grown
    beta = new / old
    doubt_ref[0, 0] = jnp.max(jnp.where(new < 0.01 * (old + grown), 1, 0))
    step_ref[...] = jnp.concatenate([step, old], axis=0)
    wide = lambda v: jnp.concatenate([v, v], axis=1)
    d = d_ref[...]
    co_ref[...] = coeffs_ref[...] + wide(step) * d
    res = r_ref[...] - wide(step) * a_ref[...]
    ro_ref[...] = res
    do_ref[...] = res + wide(beta) * d


def step_and_update(sums, coeffs, residual, direction, applied):
    piece = jax.ShapeDtypeStruct((TGT, PIECE), F32)
    return pl.pallas_call(
        step_kernel,
        out_shape=(
            piece, piece, piece,
            jax.ShapeDtypeStruct((2 * TGT, 128), F32),
            jax.ShapeDtypeStruct((1, 1), jnp.int32),
        ),
        out_specs=(
            pl.BlockSpec(memory_space=pltpu.VMEM),
            pl.BlockSpec(memory_space=pltpu.VMEM),
            pl.BlockSpec(memory_space=pltpu.VMEM),
            pl.BlockSpec(memory_space=pltpu.VMEM),
            pl.BlockSpec(memory_space=pltpu.SMEM),
        ),
    )(sums, coeffs, residual, direction, applied)


def exchange(x, axes):
    return lax.all_to_all(x, axes, 0, 0, tiled=False)


def shards(episodes, centers, coeffs, residual, direction):
    place = jnp.int32(0)
    for a in EP:
        pos = jnp.int32(0) if a in SPLIT else lax.axis_index(a)
        place = place * SIZE[a] + pos
    grid = jnp.zeros((1,), jnp.int32)
    for a in EP:
        step = jnp.arange(SIZE[a], dtype=jnp.int32) if a in SPLIT else jnp.zeros((1,), jnp.int32)
        grid = (grid[:, None] * SIZE[a] + step[None, :]).reshape(-1)
    blocks = place + grid

    dir_half = direction.astype(BF16)
    dirs = exchange(jnp.broadcast_to(dir_half, (N_SPLIT, TGT, PIECE)), SPLIT)
    eps = exchange(jnp.broadcast_to(episodes, (N_MERGED, F, 512)), MERGED)
    kmat = tiles(blocks, eps, centers)
    row_parts = exchange(row_sums(dirs, kmat), ROWS)
    rows = exchange(spread(row_parts), ROWS)
    parts = exchange(column_sums(rows, kmat), SPLIT)
    applied, sums = apply_and_sum(parts, residual, direction)
    sums = exchange(sums.reshape(256, 1, 4 * TGT), AXES).reshape(256, 4 * TGT)
    coeffs_next, residual_next, direction_next, step, doubt = step_and_update(
        sums, coeffs, residual, direction, applied
    )

    def summed(_):
        new = lax.psum(jnp.sum(residual_next * residual_next, axis=1), AXES)
        return residual_next + (new / step[TGT:, 0])[:, None] * direction

    direction_next = lax.cond(doubt[0, 0] > 0, summed, lambda _: direction_next, 0)
    return coeffs_next, residual_next, direction_next


def solution(mesh):
    fine = Mesh(mesh.devices.reshape(SIZES), AXES)
    piece = P(None, CTR + EP)
    return jax.shard_map(
        shards,
        mesh=fine,
        in_specs=(P(None, EP), P(None, CTR), piece, piece, piece),
        out_specs=(piece, piece, piece),
        check_vma=False,
    )
```

time: 692 us -> 145 us (0.21)
  waiting for transfers between devices: 416 us -> 5.48 us
  blocking collectives: 212 us -> 69.4 us
  Pallas kernels: 0 us -> 45.1 us
  matrix products: 40.2 us -> 0 us
  starting transfers between devices: 0.08 us -> 16.4 us
  between operations: 14.1 us -> 1.25 us
    reduce_scatter x1 -> x0, waiting for transfers between devices: 311 us -> none  [shards(): lax.psum_scatter(col_terms, 'ep', scatter_dimension=1, tiled=True)]
    psum x3 -> x0, blocking collectives: 212 us -> none  [the longest x1 125 us: shards(): old_norm = lax.psum(jnp.sum(residual * residual, axis=1), ('ep', 'ctr'))]
    all_gather x1 -> x0, waiting for transfers between devices: 105 us -> none  [shards(): piece = lax.all_gather(dir_half, 'ep', axis=1, tiled=True)]
    all_to_all x0 -> x4, blocking collectives: none -> 69.4 us  [exchange(): return lax.all_to_all(x, axes, 0, 0, tiled=False)]
    pallas_call x0 -> x6, Pallas kernels: none -> 45.1 us  [the longest x1 14.1 us: row_sums(): pl.pallas_call(row_kernel, grid=(N_SPLIT,), in_specs=[pl.BlockSpec((1, TG...]
    dot_general x16 -> x0, matrix products: 40.2 us -> none  [the longest x8 21.2 us: advance(): lax.dot_general(column_part, kernel, (((1,), (1,)), ((), ())), preferred_...]
    all_to_all x0 -> x2, starting transfers between devices: none -> 16.4 us  [exchange(): return lax.all_to_all(x, axes, 0, 0, tiled=False)]
  transfers between devices with their start and end apart: 2 -> 2, of which waited for: 2 -> 1; matrix products, arithmetic and copies ran while one was open for 1% -> 1% of each run, Pallas kernels for 0% -> 9%
where the time goes in v1:
time: 145 us; the launch traced here: 143 us
  blocking collectives  69.4 us (48%)
  Pallas kernels  45.1 us (31%)
  starting transfers between devices  16.4 us (11%)
  waiting for transfers between devices  5.48 us (4%)
  local copies, waits for them, and re-layouts  4.98 us (3%)
    all_to_all x4, blocking collectives, exchange(): return lax.all_to_all(x, axes, 0, 0, tiled=False)  69.4 us
    all_to_all x2, starting transfers between devices, exchange(): return lax.all_to_all(x, axes, 0, 0, tiled=False)  16.4 us
    pallas_call x1, Pallas kernels, row_sums(): pl.pallas_call(row_kernel, grid=(N_SPLIT,), in_specs=[pl.BlockSpec((1, TG...  14.1 us
    pallas_call x1, Pallas kernels, column_sums(): pl.pallas_call(column_kernel, grid=(N_SPLIT,), in_specs=[pl.BlockSpec((N_...  13 us
    pallas_call x1, Pallas kernels, tiles(): pl.pallas_call(tile_kernel, grid_spec=pltpu.PrefetchScalarGridSpec(num_sc...  12.8 us
    all_to_all x2, waiting for transfers between devices, exchange(): return lax.all_to_all(x, axes, 0, 0, tiled=False)  5.48 us
  transfers between devices with their start and end apart: 2, of which 1 were waited for; matrix products, arithmetic and copies ran while one was open for 1% of the time, Pallas kernels for 9%

profile of v1, /device:TPU:1, one launch (start us, length us, event | category | flops | bytes accessed | tf_op | source)
XLA Modules:
  0.0 143.5 jit_solution(7523916202429364333)
XLA Ops:
  0.6 1.7 %broadcast_in_dim.9 = bf16[4,96,512]{2,1,0:T(8,128)(2,1)} broadcast(bf16[96,512]{1,0:T(8,128)(2,1)} %param.7), dimensions={1,2} | broadcast | bytes 491520 | tf_op jit(solution)/shard_map/broadcast_in_dim | solution.py:232
  2.3 4.8 %all-to-all-start.1 = ((bf16[4,96,512]{2,1,0:T(8,128)(2,1)}), bf16[4,96,512]{2,1,0:T(8,128)(2,1)S(1)}, u32[]{:S(2)}, u32[]{:S(2)}) async-start(bf16[4,96,512]{2,1,0:T(8,128)(2,1)} %broadcast_in_dim.9), calls=%async_computation.1 | async-start | bytes 786432 | tf_op jit(solution)/shard_map/all_to_all | solution.py:216
  7.1 0.8 convert_element_type.9
  7.9 5.5 %all-to-all-done.1.eps_ref = bf16[4,96,512]{2,1,0:T(8,128)(2,1)S(1)} async-done(((bf16[4,96,512]{2,1,0:T(8,128)(2,1)}), bf16[4,96,512]{2,1,0:T(8,128)(2,1)S(1)}, u32[]{:S(2)}, u32[]{:S(2)}) %all-to-all-start.1) | async-done | bytes 393248 | tf_op jit(solution)/shard_map/all_to_all | solution.py:216
  13.4 0.7 broadcast_in_dim.8
  14.1 11.6 %all-to-all-start = ((bf16[16,32,256]{2,1,0:T(8,128)(2,1)}), bf16[16,32,256]{2,1,0:T(8,128)(2,1)S(1)}, u32[]{:S(2)}, u32[]{:S(2)}) async-start(bf16[16,32,256]{2,1,0:T(8,128)(2,1)} %broadcast_in_dim.8), calls=%async_computation | async-start | bytes 524288 | tf_op jit(solution)/shard_map/all_to_all | solution.py:216
  25.7 0.1 multiply_add_fusion.1
  25.7 0.1 add.35.blocks
  25.8 0.0 copy-start
  25.8 1.9 %copy-done = bf16[96,16384]{1,0:T(8,128)(2,1)S(1)} copy-done((bf16[96,16384]{1,0:T(8,128)(2,1)S(1)}, bf16[96,16384]{1,0:T(8,128)(2,1)}, u32[]{:S(2)}) %copy-start) | copy-done | bytes 3145752
  27.7 12.8 %shard_map.76.k_ref = bf16[16,2048,256]{2,1,0:T(8,128)(2,1)} custom-call(s32[16]{0:T(128)S(1)} %add.35.blocks, bf16[4,96,512]{2,1,0:T(8,128)(2,1)S(1)} %all-to-all-done.1.eps_ref, bf16[96,16384]{1,0:T(8,128)(2,1)S(1)} %copy-done), custom_call_target="tpu_custom_call" | custom-call | flops 2147483648 | bytes 16777216 | tf_op jit(solution)/shard_map/pallas_call | solution.py:71
  40.5 0.0 all-to-all-done.d_ref
  40.5 14.1 %shard_map.77 = f32[16,32,128]{2,1,0:T(8,128)S(1)} custom-call(bf16[16,32,256]{2,1,0:T(8,128)(2,1)S(1)} %all-to-all-done.d_ref, bf16[16,2048,256]{2,1,0:T(8,128)(2,1)} %shard_map.76.k_ref), custom_call_target="tpu_custom_call" | custom-call | flops 536870912 | bytes 16777216 | tf_op jit(solution)/shard_map/pallas_call | solution.py:107
  54.6 13.0 %all_to_all.30.parts_ref = f32[16,32,128]{2,1,0:T(8,128)} all-to-all(f32[16,32,128]{2,1,0:T(8,128)S(1)} %shard_map.77), channel_id=1, replica_groups=mesh['yh'=2,'z'=8,'x'=4,'yl'=2,'c'=2] {'x','yl','c'}, dimensions={0} | all-to-all | bytes 524288 | tf_op jit(solution)/shard_map/all_to_all | solution.py:216
  67.6 1.6 %shard_map.78 = bf16[16,32,128]{2,1,0:T(8,128)(2,1)} custom-call(f32[16,32,128]{2,1,0:T(8,128)} %all_to_all.30.parts_ref), custom_call_target="tpu_custom_call" | custom-call | tf_op jit(solution)/shard_map/pallas_call | solution.py:129
  69.3 9.9 %all_to_all.31.rows_ref = bf16[16,32,128]{2,1,0:T(8,128)(2,1)S(1)} all-to-all(bf16[16,32,128]{2,1,0:T(8,128)(2,1)} %shard_map.78), channel_id=1, replica_groups=mesh['yh'=2,'z'=8,'x'=4,'yl'=2,'c'=2] {'x','yl','c'}, dimensions={0} | all-to-all | bytes 262144 | tf_op jit(solution)/shard_map/all_to_all | solution.py:216
  79.2 13.0 %shard_map.79 = f32[16,32,256]{2,1,0:T(8,128)S(1)} custom-call(bf16[16,32,128]{2,1,0:T(8,128)(2,1)S(1)} %all_to_all.31.rows_ref, bf16[16,2048,256]{2,1,0:T(8,128)(2,1)} %shard_map.76.k_ref), custom_call_target="tpu_custom_call" | custom-call | flops 536870912 | bytes 16777216 | tf_op jit(solution)/shard_map/pallas_call | solution.py:144
  92.2 24.0 %all_to_all.32.parts_ref = f32[16,32,256]{2,1,0:T(8,128)} all-to-all(f32[16,32,256]{2,1,0:T(8,128)S(1)} %shard_map.79), channel_id=1, replica_groups=mesh['yh'=2,'z'=8,'x'=4,'yl'=2,'c'=2] {'yh','z'}, dimensions={0} | all-to-all | bytes 1048576 | tf_op jit(solution)/shard_map/all_to_all | solution.py:216
  116.1 0.0 copy-done.1
  116.1 1.8 %shard_map.80 = (f32[32,256]{1,0:T(8,128)}, f32[256,128]{1,0:T(8,128)}) custom-call(f32[16,32,256]{2,1,0:T(8,128)} %all_to_all.32.parts_ref, f32[32,256]{1,0:T(8,128)} %r_ref.3, f32[32,256]{1,0:T(8,128)S(1)} %copy-done.1), custom_call_target="tpu_custom_call" | custom-call | tf_op jit(solution)/shard_map/pallas_call | solution.py:169
  118.0 22.5 %all_to_all.33 = f32[256,1,128]{2,1,0:T(1,128)} all-to-all(f32[256,1,128]{2,1,0:T(1,128)} %bitcast.10), channel_id=1, replica_groups=mesh['yh'=2,'z'=8,'x'=4,'yl'=2,'c'=2] {'yh','z','x','yl','c'}, dimensions={0} | all-to-all | bytes 262144 | tf_op jit(solution)/shard_map/all_to_all | solution.py:216
  140.5 1.8 %shard_map.81 = (f32[32,256]{1,0:T(8,128)}, f32[32,256]{1,0:T(8,128)}, f32[32,256]{1,0:T(8,128)S(1)}, f32[64,128]{1,0:T(8,128)S(1)}, s32[1,1]{1,0:T(1,128)}) custom-call(f32[256,128]{1,0:T(8,128)} %bitcast.9, f32[32,256]{1,0:T(8,128)} %coeffs_ref.1, f32[32,256]{1,0:T(8,128)} %r_ref.3, f32[32,256]{1,0:T(8,128)S(1)} %copy-done.1, ...), custom_call_target="tpu_custom_call" | custom-call | tf_op jit(solution)/shard_map/pallas_call | solution.py:198
  142.9 0.0 copy-start.2
  142.9 0.6 copy-done.2
  (3 shorter events, 0.0 us)
Async XLA Ops:
  2.3 11.1 %all-to-all-start.1 = ((bf16[4,96,512]{2,1,0:T(8,128)(2,1)}), bf16[4,96,512]{2,1,0:T(8,128)(2,1)S(1)}, u32[]{:S(2)}, u32[]{:S(2)}) async-start(bf16[4,96,512]{2,1,0:T(8,128)(2,1)} %broadcast_in_dim.9), calls=%async_computation.1 | async-start | bytes 786432 | tf_op jit(solution)/shard_map/all_to_all | solution.py:216
  14.1 26.4 %all-to-all-start = ((bf16[16,32,256]{2,1,0:T(8,128)(2,1)}), bf16[16,32,256]{2,1,0:T(8,128)(2,1)S(1)}, u32[]{:S(2)}, u32[]{:S(2)}) async-start(bf16[16,32,256]{2,1,0:T(8,128)(2,1)} %broadcast_in_dim.8), calls=%async_computation | async-start | bytes 524288 | tf_op jit(solution)/shard_map/all_to_all | solution.py:216
  25.8 1.9 %copy-start = (bf16[96,16384]{1,0:T(8,128)(2,1)S(1)}, bf16[96,16384]{1,0:T(8,128)(2,1)}, u32[]{:S(2)}) copy-start(bf16[96,16384]{1,0:T(8,128)(2,1)} %cen_ref.1) | copy-start | bytes 9437188
  40.5 75.7 %copy-start.1 = (f32[32,256]{1,0:T(8,128)S(1)}, f32[32,256]{1,0:T(8,128)}, u32[]{:S(2)}) copy-start(f32[32,256]{1,0:T(8,128)} %d_ref.3) | copy-start | bytes 98308
  142.9 0.6 copy-start.2

commit v2 on v1

v2 whole, which is shorter than its diff:
```python
import jax
import jax.numpy as jnp
from jax import lax
from jax.experimental import pallas as pl
from jax.experimental.pallas import tpu as pltpu
from jax.sharding import Mesh, PartitionSpec as P

AXES = ("yh", "zh", "zm", "zl", "x", "yl", "c")
SIZES = (2, 2, 2, 2, 4, 2, 2)
SIZE = dict(zip(AXES, SIZES))
EP = ("yh", "zh", "zm", "zl", "x")
CTR = ("yl", "c")
SPLIT = ("yh", "zh", "zm", "zl")
MERGED = tuple(a for a in EP if a not in SPLIT)
ROWS = MERGED + CTR

F = 96
DEPTH = 128
TGT = 32
PIECE = 256
ROWPIECE = 128
OWN = 512
SHARP = 3.0 / F
F32 = jnp.float32
BF16 = jnp.bfloat16
IN_VMEM = pl.BlockSpec(memory_space=pltpu.VMEM)
IN_SMEM = pl.BlockSpec(memory_space=pltpu.SMEM)


def prod(axes):
    out = 1
    for a in axes:
        out *= SIZE[a]
    return out


def places(axes):
    out = [0]
    for a in EP:
        out = [p * SIZE[a] + k for p in out for k in range(SIZE[a] if a in axes else 1)]
    return out


N_SPLIT, N_MERGED, N_ROWS = prod(SPLIT), prod(MERGED), prod(ROWS)
N_EP = OWN * N_MERGED
BLOCKS = places(SPLIT)


def params(mib):
    return pltpu.CompilerParams(vmem_limit_bytes=mib * 1024 * 1024)


def here(x):
    return pltpu.with_memory_space_constraint(x, pltpu.VMEM)


def exchange(x, axes):
    return here(lax.all_to_all(here(x), axes, 0, 0, tiled=False))


def three(v):
    hi = v.astype(BF16).astype(F32)
    mid = (v - hi).astype(BF16).astype(F32)
    return hi, mid, v - hi - mid


def extra_rows(norm_parts, first, width):
    row = lax.broadcasted_iota(jnp.int32, (DEPTH - F, width), 0)
    out = jnp.where(row < 6, 1.0, 0.0).astype(F32)
    for k, part in enumerate(norm_parts):
        out = jnp.where(row == first + k, part, out)
    return out


def copies_kernel(d_ref, out_ref):
    half = d_ref[...].astype(BF16)
    for i in range(N_SPLIT):
        out_ref[i] = half


def copies(direction):
    return pl.pallas_call(
        copies_kernel, out_shape=pltpu.VMEM((N_SPLIT, TGT, PIECE), BF16), compiler_params=params(4)
    )(direction)


UNROLL = 4


def tile_kernel(*refs):
    place_ref, slot_ref = refs[:2]
    eps_refs = refs[2:2 + N_MERGED]
    cen_ref, d_ref, k_ref, out_ref, left, cens, own, sems = refs[2 + N_MERGED:]

    def fetch(i):
        start = pl.multiple_of((place_ref[0] + BLOCKS[i]) * PIECE, PIECE)
        return pltpu.make_async_copy(cen_ref.at[:, pl.ds(start, PIECE)], cens.at[i], sems.at[i])

    mine = pltpu.make_async_copy(eps_refs[0], own, sems.at[N_SPLIT])
    mine.start()
    for i in range(N_SPLIT):
        fetch(i).start()
    for m in reversed(range(N_MERGED)):
        if m == 0:
            mine.wait()
        e = (eps_refs[m] if m else own)[...].astype(F32)
        norm = jnp.sum(e * e, axis=0, keepdims=True)
        tall = jnp.concatenate([e * (2.0 * SHARP), extra_rows(three(-SHARP * norm), 0, OWN)], axis=0)
        slot = pl.multiple_of((slot_ref[0] ^ m) * OWN, OWN)
        left[pl.ds(slot, OWN), :] = tall.T.astype(BF16)
    for i in range(N_SPLIT):
        fetch(i).wait()

    def block(i):
        c = cens[i].astype(F32)
        norm = jnp.sum(c * c, axis=0, keepdims=True)
        right = jnp.concatenate([cens[i], extra_rows(three(-SHARP * norm), 3, PIECE).astype(BF16)], axis=0)
        for r in range(0, N_EP, 256):
            arg = jnp.dot(left[r:r + 256, :], right, preferred_element_type=F32)
            k_ref[i, r:r + 256, :] = jnp.exp(arg).astype(BF16)

    def step(n, carry):
        for u in range(UNROLL):
            block(n * UNROLL + u)
        return carry

    lax.fori_loop(0, N_SPLIT // UNROLL, step, 0)

    for r in range(0, N_EP, 512):
        total = None
        for i in range(N_SPLIT):
            part = lax.dot_general(
                k_ref[i, r:r + 512, :], d_ref[i], (((1,), (1,)), ((), ())), preferred_element_type=F32
            )
            total = part if total is None else total + part
        total = total.T
        for j in range(512 // ROWPIECE):
            out_ref[r // ROWPIECE + j] = total[:, j * ROWPIECE:(j + 1) * ROWPIECE]


def tiles_and_rows(place, slot, eps, centers, dirs):
    in_hbm = lambda x: pltpu.with_memory_space_constraint(x, pltpu.HBM)
    anywhere = pl.BlockSpec(memory_space=pl.ANY)
    return pl.pallas_call(
        tile_kernel,
        in_specs=[IN_SMEM] * 2 + [anywhere] + [IN_VMEM] * (N_MERGED - 1) + [anywhere, IN_VMEM],
        out_specs=(IN_VMEM, IN_VMEM),
        out_shape=(pltpu.VMEM((N_SPLIT, N_EP, PIECE), BF16), pltpu.VMEM((N_ROWS, TGT, ROWPIECE), F32)),
        scratch_shapes=[
            pltpu.VMEM((N_EP, DEPTH), BF16),
            pltpu.VMEM((N_SPLIT, F, PIECE), BF16),
            pltpu.VMEM((F, OWN), BF16),
            pltpu.SemaphoreType.DMA((N_SPLIT + 1,)),
        ],
        compiler_params=params(24),
        cost_estimate=pl.CostEstimate(
            flops=2 * (DEPTH + TGT) * 2 ** 23, bytes_accessed=2 ** 24, transcendentals=2 ** 23
        ),
    )(place, slot, in_hbm(eps[0]), *eps[1:], in_hbm(centers), dirs)


def spread_kernel(parts_ref, out_ref):
    half = jnp.sum(parts_ref[...], axis=0).astype(BF16)
    for j in range(N_ROWS):
        out_ref[j] = half


def spread(parts):
    return pl.pallas_call(
        spread_kernel, out_shape=pltpu.VMEM((N_ROWS, TGT, ROWPIECE), BF16), compiler_params=params(4)
    )(parts)


def column_kernel(rows_ref, k_ref, out_ref, half):
    for j in range(N_ROWS):
        half[:, j * ROWPIECE:(j + 1) * ROWPIECE] = rows_ref[j]
    for i in range(N_SPLIT):
        out_ref[i] = jnp.dot(half[...], k_ref[i], preferred_element_type=F32)


def column_sums(rows, kmat):
    return pl.pallas_call(
        column_kernel,
        in_specs=[IN_VMEM] * 2,
        out_specs=IN_VMEM,
        out_shape=pltpu.VMEM((N_SPLIT, TGT, PIECE), F32),
        scratch_shapes=[pltpu.VMEM((TGT, N_EP), BF16)],
        compiler_params=params(8),
        cost_estimate=pl.CostEstimate(flops=2 * TGT * 2 ** 23, bytes_accessed=2 ** 24, transcendentals=0),
    )(rows, here(kmat))


def lane_sums(v):
    return jnp.broadcast_to(jnp.sum(v, axis=1, keepdims=True), (TGT, 128))


def wide(v):
    return jnp.concatenate([v, v], axis=1)


def apply_kernel(parts_ref, r_ref, d_ref, applied_ref, sums_ref):
    r, d = r_ref[...], d_ref[...]
    a = jnp.sum(parts_ref[...], axis=0) + 1.0 * d
    applied_ref[...] = a
    aa = lane_sums(a * a)
    fit = jnp.where(aa > 0.0, lane_sums(r * a) / jnp.where(aa > 0.0, aa, 1.0), 0.0)
    rest = r - wide(fit) * a
    cols = jnp.concatenate([lane_sums(rest * rest), fit, aa, lane_sums(d * a)], axis=0)
    sums_ref[...] = jnp.broadcast_to(cols.T[:1], sums_ref.shape)


def apply_and_sum(parts, residual, direction):
    return pl.pallas_call(
        apply_kernel,
        out_shape=(pltpu.VMEM((TGT, PIECE), F32), jax.ShapeDtypeStruct((256, 4 * TGT), F32)),
        compiler_params=params(4),
    )(parts, residual, direction)


def step_kernel(sums_ref, coeffs_ref, r_ref, d_ref, a_ref, co_ref, ro_ref, do_ref):
    rest, fit, aa, da = (sums_ref[:, k * TGT:(k + 1) * TGT] for k in range(4))
    old = jnp.sum(rest + fit * (fit * aa), axis=0, keepdims=True)
    step = old / jnp.sum(da, axis=0, keepdims=True)
    off = step - fit
    new = jnp.sum(rest + off * (off * aa), axis=0, keepdims=True)
    step = wide(jnp.broadcast_to(step, (128, TGT)).T)
    beta = wide(jnp.broadcast_to(new / old, (128, TGT)).T)
    d = d_ref[...]
    co_ref[...] = coeffs_ref[...] + step * d
    res = r_ref[...] - step * a_ref[...]
    ro_ref[...] = res
    do_ref[...] = res + beta * d


def step_and_update(sums, coeffs, residual, direction, applied):
    return pl.pallas_call(
        step_kernel,
        out_shape=(jax.ShapeDtypeStruct((TGT, PIECE), F32),) * 3,
        compiler_params=params(4),
    )(sums, coeffs, residual, direction, here(applied))


def swaps(x):
    pairs = lambda m: [(k, k ^ m) for k in range(N_MERGED)]
    return [x] + [lax.ppermute(x, MERGED, pairs(m)) for m in range(1, N_MERGED)]


def shards(episodes, centers, coeffs, residual, direction):
    place = jnp.int32(0)
    slot = jnp.int32(0)
    for a in EP:
        if a in SPLIT:
            place = place * SIZE[a]
        else:
            place = place * SIZE[a] + lax.axis_index(a)
            slot = slot * SIZE[a] + lax.axis_index(a)

    eps = swaps(episodes)
    dirs = exchange(copies(direction), SPLIT)
    kmat, row_parts = tiles_and_rows(place.reshape(1), slot.reshape(1), eps, centers, dirs)
    row_parts = exchange(row_parts, ROWS)
    rows = exchange(spread(row_parts), ROWS)
    parts = exchange(column_sums(rows, kmat), SPLIT)
    applied, sums = apply_and_sum(parts, residual, direction)
    sums = lax.all_to_all(sums.reshape(256, 1, 4 * TGT), AXES, 0, 0, tiled=False).reshape(256, 4 * TGT)
    return step_and_update(sums, coeffs, residual, direction, applied)


def solution(mesh):
    fine = Mesh(mesh.devices.reshape(SIZES), AXES)
    piece = P(None, CTR + EP)
    return jax.shard_map(
        shards,
        mesh=fine,
        in_specs=(P(None, EP), P(None, CTR), piece, piece, piece),
        out_specs=(piece, piece, piece),
        check_vma=False,
    )
```

time: 145 us -> 105 us (0.72); the launches traced: 143 us -> 105 us
  Pallas kernels: 45.1 us -> 15.8 us
  local copies, waits for them, and re-layouts: 4.98 us -> 0.76 us
  blocking collectives: 69.4 us -> 65.8 us
    pallas_call x6, Pallas kernels: 45.1 us -> 15.8 us  [the longest x1 10.9 us: tiles_and_rows(): pl.pallas_call(tile_kernel, in_specs=[IN_SMEM] * 2 + [anywhere] + [IN_VME...]
    ppermute x0 -> x3, waiting for transfers between devices: none -> 4.85 us  [swaps(): return [x] + [lax.ppermute(x, MERGED, pairs(m)) for m in range(1, N_MERGED)]]
    all_to_all x2 -> x1, starting transfers between devices: 16.4 us -> 11.7 us  [exchange(): return here(lax.all_to_all(here(x), axes, 0, 0, tiled=False))]
    all_to_all x2 -> x1, waiting for transfers between devices: 5.48 us -> 1.68 us  [exchange(): return here(lax.all_to_all(here(x), axes, 0, 0, tiled=False))]
    ppermute x0 -> x3, starting transfers between devices: none -> 3.69 us  [swaps(): return [x] + [lax.ppermute(x, MERGED, pairs(m)) for m in range(1, N_MERGED)]]
    all_to_all x4, blocking collectives: 69.4 us -> 65.8 us  [the longest x3 44 us: exchange(): return here(lax.all_to_all(here(x), axes, 0, 0, tiled=False))]
    broadcast_in_dim x2 -> x0, local copies, waits for them, and re-layouts: 2.39 us -> none  [the longest x1 1.66 us: shards(): eps = exchange(jnp.broadcast_to(episodes, (N_MERGED, F, 512)), MERGED)]
    unnamed x6 -> x8, local copies, waits for them, and re-layouts: 2.5 us -> 0.76 us
  transfers between devices with their start and end apart: 2 -> 4, of which waited for: 1 -> 4; matrix products, arithmetic and copies ran while one was open for 1% -> 0% of each run, Pallas kernels for 9% -> 0%
where the time goes in v2:
time: 105 us
  blocking collectives  65.8 us (63%)
  Pallas kernels  15.8 us (15%)
  starting transfers between devices  15.4 us (15%)
  waiting for transfers between devices  6.54 us (6%)
    all_to_all x3, blocking collectives, exchange(): return here(lax.all_to_all(here(x), axes, 0, 0, tiled=False))  44 us
    all_to_all x1, blocking collectives, shards(): lax.all_to_all(sums.reshape(256, 1, 4 * TGT), AXES, 0, 0, tiled=False)  21.8 us
    all_to_all x1, starting transfers between devices, exchange(): return here(lax.all_to_all(here(x), axes, 0, 0, tiled=False))  11.7 us
    pallas_call x1, Pallas kernels, tiles_and_rows(): pl.pallas_call(tile_kernel, in_specs=[IN_SMEM] * 2 + [anywhere] + [IN_VME...  10.9 us
    ppermute x3, waiting for transfers between devices, swaps(): return [x] + [lax.ppermute(x, MERGED, pairs(m)) for m in range(1, N_MERGED)]  4.85 us
    ppermute x3, starting transfers between devices, swaps(): return [x] + [lax.ppermute(x, MERGED, pairs(m)) for m in range(1, N_MERGED)]  3.69 us
    pallas_call x1, Pallas kernels, column_sums(): pl.pallas_call(column_kernel, in_specs=[IN_VMEM] * 2, out_specs=IN_VMEM,...  2.97 us
  transfers between devices with their start and end apart: 4, of which 4 were waited for; matrix products, arithmetic and copies ran while one was open for 0% of the time, Pallas kernels for 0%

profile of v2, /device:TPU:1, one launch (start us, length us, event | category | flops | bytes accessed | tf_op | source)
XLA Modules:
  0.0 105.0 jit_solution(7828702412088974022)
XLA Ops:
  0.6 0.0 copy-start
  0.6 0.7 copy-done
  1.4 0.7 shard_map.76
  2.1 11.7 %all-to-all-start = ((bf16[16,32,256]{2,1,0:T(8,128)(2,1)}), bf16[16,32,256]{2,1,0:T(8,128)(2,1)S(1)}, u32[]{:S(2)}, u32[]{:S(2)}) async-start(bf16[16,32,256]{2,1,0:T(8,128)(2,1)} %shard_map.76), calls=%async_computation | async-start | bytes 524288 | tf_op jit(solution)/shard_map/all_to_all | solution.py:58
  13.9 2.8 %collective-permute-start.1 = (bf16[96,512]{1,0:T(8,128)(2,1)}, bf16[96,512]{1,0:T(8,128)(2,1)S(1)}, u32[]{:S(2)}, u32[]{:S(2)}) collective-permute-start(bf16[96,512]{1,0:T(8,128)(2,1)} %refs_2_.1), channel_id=1, source_target_pairs={{0,8},{4,12},{8,0},{12,4},{1,9},{5,13},{9,1},{13,5},{2,10},{6,14},... | collective-permute-start | bytes 294920 | tf_op jit(solution)/shard_map/ppermute | solution.py:245
  16.7 0.3 collective-permute-start
  17.0 0.6 collective-permute-start.2
  17.6 1.6 %collective-permute-done.1.refs_4_ = bf16[96,512]{1,0:T(8,128)(2,1)S(1)} collective-permute-done((bf16[96,512]{1,0:T(8,128)(2,1)}, bf16[96,512]{1,0:T(8,128)(2,1)S(1)}, u32[]{:S(2)}, u32[]{:S(2)}) %collective-permute-start.1) | collective-permute-done | bytes 98336 | tf_op jit(solution)/shard_map/ppermute | solution.py:245
  19.2 2.3 %collective-permute-done.refs_3_ = bf16[96,512]{1,0:T(8,128)(2,1)S(1)} collective-permute-done((bf16[96,512]{1,0:T(8,128)(2,1)}, bf16[96,512]{1,0:T(8,128)(2,1)S(1)}, u32[]{:S(2)}, u32[]{:S(2)}) %collective-permute-start) | collective-permute-done | bytes 98336 | tf_op jit(solution)/shard_map/ppermute | solution.py:245
  21.5 1.0 collective-permute-done.2.refs_5_
  22.4 1.7 %all-to-all-done.refs_7_ = bf16[16,32,256]{2,1,0:T(8,128)(2,1)S(1)} async-done(((bf16[16,32,256]{2,1,0:T(8,128)(2,1)}), bf16[16,32,256]{2,1,0:T(8,128)(2,1)S(1)}, u32[]{:S(2)}, u32[]{:S(2)}) %all-to-all-start) | async-done | bytes 262176 | tf_op jit(solution)/shard_map/all_to_all | solution.py:58
  24.1 0.0 copy-start.1
  24.1 0.0 copy-start.2
  24.1 10.9 %shard_map.77 = (bf16[16,2048,256]{2,1,0:T(8,128)(2,1)S(1)}, f32[16,32,128]{2,1,0:T(8,128)S(1)}) custom-call(s32[1]{0:T(128)} %bitcast.refs_0_.refs_1_, s32[1]{0:T(128)} %bitcast.refs_0_.refs_1_, bf16[96,512]{1,0:T(8,128)(2,1)} %refs_2_.1, bf16[96,512]{1,0:T(8,128)(2,1)S(1)} %collective-permute-done.refs_3_, ...), custom_call_target="tpu_custom_call" | custom-call | flops 2684354560 | bytes 16777216 | tf_op jit(solution)/shard_map/pallas_call | solution.py:144
  35.1 14.0 %all_to_all.25.parts_ref = f32[16,32,128]{2,1,0:T(8,128)S(1)} all-to-all(f32[16,32,128]{2,1,0:T(8,128)S(1)} %get-tuple-element.7), channel_id=1, replica_groups=mesh['yh'=2,'zh'=2,'zm'=2,'zl'=2,'x'=4,'yl'=2,'c'=2] {'x','yl','c'}, dimensions={0} | all-to-all | bytes 524288 | tf_op jit(solution)/shard_map/all_to_all | solution.py:58
  49.1 9.0 %all_to_all.26.rows_ref = bf16[16,32,128]{2,1,0:T(8,128)(2,1)S(1)} all-to-all(bf16[16,32,128]{2,1,0:T(8,128)(2,1)S(1)} %shard_map.78), channel_id=1, replica_groups=mesh['yh'=2,'zh'=2,'zm'=2,'zl'=2,'x'=4,'yl'=2,'c'=2] {'x','yl','c'}, dimensions={0} | all-to-all | bytes 262144 | tf_op jit(solution)/shard_map/all_to_all | solution.py:58
  58.1 3.0 %shard_map.79 = f32[16,32,256]{2,1,0:T(8,128)S(1)} custom-call(bf16[16,32,128]{2,1,0:T(8,128)(2,1)S(1)} %all_to_all.26.rows_ref, bf16[16,2048,256]{2,1,0:T(8,128)(2,1)S(1)} %get-tuple-element.8.k_ref), custom_call_target="tpu_custom_call" | custom-call | flops 536870912 | bytes 16777216 | tf_op jit(solution)/shard_map/pallas_call | solution.py:182
  61.1 21.0 %all_to_all.27.parts_ref = f32[16,32,256]{2,1,0:T(8,128)S(1)} all-to-all(f32[16,32,256]{2,1,0:T(8,128)S(1)} %shard_map.79), channel_id=1, replica_groups=mesh['yh'=2,'zh'=2,'zm'=2,'zl'=2,'x'=4,'yl'=2,'c'=2] {'yh','zh','zm','zl'}, dimensions={0} | all-to-all | bytes 1048576 | tf_op jit(solution)/shard_map/all_to_all | solution.py:58
  82.1 0.0 copy-done.1
  82.1 0.0 copy-done.2
  82.1 0.3 shard_map.80
  82.3 21.8 %all_to_all.28 = f32[256,1,128]{2,1,0:T(1,128)S(1)} all-to-all(f32[256,1,128]{2,1,0:T(1,128)S(1)} %bitcast.6), channel_id=1, replica_groups=mesh['yh'=2,'zh'=2,'zm'=2,'zl'=2,'x'=4,'yl'=2,'c'=2] {'yh','zh','zm','zl..., dimensions={0} | all-to-all | bytes 262144 | tf_op jit(solution)/shard_map/all_to_all | solution.py:265
  104.1 0.0 copy-done.3
  104.1 0.9 shard_map.81
  (2 shorter events, 0.0 us)
Async XLA Ops:
  0.6 0.8 copy-start
  2.1 22.0 %all-to-all-start = ((bf16[16,32,256]{2,1,0:T(8,128)(2,1)}), bf16[16,32,256]{2,1,0:T(8,128)(2,1)S(1)}, u32[]{:S(2)}, u32[]{:S(2)}) async-start(bf16[16,32,256]{2,1,0:T(8,128)(2,1)} %shard_map.76), calls=%async_computation | async-start | bytes 524288 | tf_op jit(solution)/shard_map/all_to_all | solution.py:58
  13.9 5.3 %collective-permute-start.1 = (bf16[96,512]{1,0:T(8,128)(2,1)}, bf16[96,512]{1,0:T(8,128)(2,1)S(1)}, u32[]{:S(2)}, u32[]{:S(2)}) collective-permute-start(bf16[96,512]{1,0:T(8,128)(2,1)} %refs_2_.1), channel_id=1, source_target_pairs={{0,8},{4,12},{8,0},{12,4},{1,9},{5,13},{9,1},{13,5},{2,10},{6,14},... | collective-permute-start | bytes 294920 | tf_op jit(solution)/shard_map/ppermute | solution.py:245
  16.7 4.8 %collective-permute-start = (bf16[96,512]{1,0:T(8,128)(2,1)}, bf16[96,512]{1,0:T(8,128)(2,1)S(1)}, u32[]{:S(2)}, u32[]{:S(2)}) collective-permute-start(bf16[96,512]{1,0:T(8,128)(2,1)} %refs_2_.1), channel_id=1, source_target_pairs={{0,4},{4,0},{8,12},{12,8},{1,5},{5,1},{9,13},{13,9},{2,6},{6,2},{1... | collective-permute-start | bytes 294920 | tf_op jit(solution)/shard_map/ppermute | solution.py:245
  17.0 5.4 %collective-permute-start.2 = (bf16[96,512]{1,0:T(8,128)(2,1)}, bf16[96,512]{1,0:T(8,128)(2,1)S(1)}, u32[]{:S(2)}, u32[]{:S(2)}) collective-permute-start(bf16[96,512]{1,0:T(8,128)(2,1)} %refs_2_.1), channel_id=1, source_target_pairs={{0,12},{4,8},{8,4},{12,0},{1,13},{5,9},{9,5},{13,1},{2,14},{6,10},... | collective-permute-start | bytes 294920 | tf_op jit(solution)/shard_map/ppermute | solution.py:245
  24.1 57.9 %copy-start.1 = (f32[32,256]{1,0:T(8,128)S(1)}, f32[32,256]{1,0:T(8,128)}, u32[]{:S(2)}) copy-start(f32[32,256]{1,0:T(8,128)} %d_ref.5) | copy-start | bytes 98308
  24.1 57.9 %copy-start.2 = (f32[32,256]{1,0:T(8,128)S(1)}, f32[32,256]{1,0:T(8,128)}, u32[]{:S(2)}) copy-start(f32[32,256]{1,0:T(8,128)} %r_ref.3) | copy-start | bytes 98308
  24.1 80.0 %copy-start.3 = (f32[32,256]{1,0:T(8,128)S(1)}, f32[32,256]{1,0:T(8,128)}, u32[]{:S(2)}) copy-start(f32[32,256]{1,0:T(8,128)} %coeffs_ref.1) | copy-start | bytes 98308

commit v3 on v2

--- a/solution.py
+++ b/solution.py
@@ -1,3 +1,5 @@
+import functools
+
 import jax
 import jax.numpy as jnp
 from jax import lax
@@ -23,6 +25,7 @@
 SHARP = 3.0 / F
 F32 = jnp.float32
 BF16 = jnp.bfloat16
+F16 = jnp.float16
 IN_VMEM = pl.BlockSpec(memory_space=pltpu.VMEM)
 IN_SMEM = pl.BlockSpec(memory_space=pltpu.SMEM)
 
@@ -171,11 +174,23 @@
     )(parts)
 
 
+MESSAGE = 72
+HALF = PIECE // 2
+
+
 def column_kernel(rows_ref, k_ref, out_ref, half):
     for j in range(N_ROWS):
         half[:, j * ROWPIECE:(j + 1) * ROWPIECE] = rows_ref[j]
-    for i in range(N_SPLIT):
-        out_ref[i] = jnp.dot(half[...], k_ref[i], preferred_element_type=F32)
+    sums = [jnp.dot(half[...], k_ref[i], preferred_element_type=F32) for i in range(N_SPLIT)]
+    top = functools.reduce(jnp.maximum, [jnp.abs(v) for v in sums])
+    top = jnp.max(jnp.maximum(top[:, :HALF], top[:, HALF:]), axis=1, keepdims=True)
+    power = jnp.ceil(jnp.log2(jnp.maximum(jnp.broadcast_to(top, (TGT, HALF)), 1e-30)))
+    scale = jnp.exp2(15.0 - power)
+    line = jnp.concatenate([power] * (HALF // TGT), axis=0).T[:MESSAGE - 2 * TGT]
+    for i in range(N_SPLIT):
+        out_ref[i, :TGT, :] = sums[i][:, :HALF] * scale
+        out_ref[i, TGT:2 * TGT, :] = sums[i][:, HALF:] * scale
+        out_ref[i, 2 * TGT:, :] = line
 
 
 def column_sums(rows, kmat):
@@ -183,13 +198,23 @@
         column_kernel,
         in_specs=[IN_VMEM] * 2,
         out_specs=IN_VMEM,
-        out_shape=pltpu.VMEM((N_SPLIT, TGT, PIECE), F32),
+        out_shape=jax.ShapeDtypeStruct((N_SPLIT, MESSAGE, HALF), F32),
         scratch_shapes=[pltpu.VMEM((TGT, N_EP), BF16)],
         compiler_params=params(8),
         cost_estimate=pl.CostEstimate(flops=2 * TGT * 2 ** 23, bytes_accessed=2 ** 24, transcendentals=0),
     )(rows, here(kmat))
 
 
+def gathered(parts_ref):
+    low = high = 0.0
+    for i in range(N_SPLIT):
+        power = jnp.broadcast_to(parts_ref[i, 2 * TGT:2 * TGT + 1, :], (HALF, HALF)).T[:TGT]
+        back = jnp.exp2(power - 15.0)
+        low = low + parts_ref[i, :TGT, :] * back
+        high = high + parts_ref[i, TGT:2 * TGT, :] * back
+    return jnp.concatenate([low, high], axis=1)
+
+
 def lane_sums(v):
     return jnp.broadcast_to(jnp.sum(v, axis=1, keepdims=True), (TGT, 128))
 
@@ -200,7 +225,7 @@
 
 def apply_kernel(parts_ref, r_ref, d_ref, applied_ref, sums_ref):
     r, d = r_ref[...], d_ref[...]
-    a = jnp.sum(parts_ref[...], axis=0) + 1.0 * d
+    a = gathered(parts_ref) + 1.0 * d
     applied_ref[...] = a
     aa = lane_sums(a * a)
     fit = jnp.where(aa > 0.0, lane_sums(r * a) / jnp.where(aa > 0.0, aa, 1.0), 0.0)
@@ -260,7 +285,8 @@
     kmat, row_parts = tiles_and_rows(place.reshape(1), slot.reshape(1), eps, centers, dirs)
     row_parts = exchange(row_parts, ROWS)
     rows = exchange(spread(row_parts), ROWS)
-    parts = exchange(column_sums(rows, kmat), SPLIT)
+    parts = column_sums(rows, kmat).astype(F16)
+    parts = lax.all_to_all(parts, SPLIT, 0, 0, tiled=False).astype(F32)
     applied, sums = apply_and_sum(parts, residual, direction)
     sums = lax.all_to_all(sums.reshape(256, 1, 4 * TGT), AXES, 0, 0, tiled=False).reshape(256, 4 * TGT)
     return step_and_update(sums, coeffs, residual, direction, applied)

time: 105 us -> 101 us (0.962)
  blocking collectives: 65.8 us -> 60.8 us
    all_to_all x3 -> x2, blocking collectives: 44 us -> 23 us  [exchange(): return here(lax.all_to_all(here(x), axes, 0, 0, tiled=False))]
    all_to_all x0 -> x1, blocking collectives: none -> 17 us  [shards(): parts = lax.all_to_all(parts, SPLIT, 0, 0, tiled=False).astype(F32)]
where the time goes in v3:
time: 101 us
  blocking collectives  60.8 us (60%)
  Pallas kernels  16.3 us (16%)
  starting transfers between devices  15.4 us (15%)
  waiting for transfers between devices  6.54 us (6%)
    all_to_all x2, blocking collectives, exchange(): return here(lax.all_to_all(here(x), axes, 0, 0, tiled=False))  23 us
    all_to_all x1, blocking collectives, shards(): lax.all_to_all(sums.reshape(256, 1, 4 * TGT), AXES, 0, 0, tiled=False)  20.9 us
    all_to_all x1, blocking collectives, shards(): parts = lax.all_to_all(parts, SPLIT, 0, 0, tiled=False).astype(F32)  17 us
    all_to_all x1, starting transfers between devices, exchange(): return here(lax.all_to_all(here(x), axes, 0, 0, tiled=False))  11.7 us
    pallas_call x1, Pallas kernels, tiles_and_rows(): pl.pallas_call(tile_kernel, in_specs=[IN_SMEM] * 2 + [anywhere] + [IN_VME...  10.9 us
    ppermute x3, waiting for transfers between devices, swaps(): return [x] + [lax.ppermute(x, MERGED, pairs(m)) for m in range(1, N_MERGED)]  4.85 us
    ppermute x3, starting transfers between devices, swaps(): return [x] + [lax.ppermute(x, MERGED, pairs(m)) for m in range(1, N_MERGED)]  3.69 us
    pallas_call x1, Pallas kernels, column_sums(): pl.pallas_call(column_kernel, in_specs=[IN_VMEM] * 2, out_specs=IN_VMEM,...  3.12 us
  transfers between devices with their start and end apart: 4, of which 4 were waited for; matrix products, arithmetic and copies ran while one was open for 0% of the time, Pallas kernels for 0%

profile of v3, /device:TPU:1, one launch (start us, length us, event | category | flops | bytes accessed | tf_op | source)
XLA Modules:
  0.0 100.6 jit_solution(15551509054370327991)
XLA Ops:
  0.6 0.0 copy-start
  0.6 0.7 copy-done
  1.4 0.7 shard_map.76
  2.1 11.7 %all-to-all-start = ((bf16[16,32,256]{2,1,0:T(8,128)(2,1)}), bf16[16,32,256]{2,1,0:T(8,128)(2,1)S(1)}, u32[]{:S(2)}, u32[]{:S(2)}) async-start(bf16[16,32,256]{2,1,0:T(8,128)(2,1)} %shard_map.76), calls=%async_computation | async-start | bytes 524288 | tf_op jit(solution)/shard_map/all_to_all | solution.py:61
  13.9 2.8 %collective-permute-start.1 = (bf16[96,512]{1,0:T(8,128)(2,1)}, bf16[96,512]{1,0:T(8,128)(2,1)S(1)}, u32[]{:S(2)}, u32[]{:S(2)}) collective-permute-start(bf16[96,512]{1,0:T(8,128)(2,1)} %refs_2_.1), channel_id=1, source_target_pairs={{0,8},{4,12},{8,0},{12,4},{1,9},{5,13},{9,1},{13,5},{2,10},{6,14},... | collective-permute-start | bytes 294920 | tf_op jit(solution)/shard_map/ppermute | solution.py:270
  16.7 0.3 collective-permute-start
  17.0 0.6 collective-permute-start.2
  17.6 1.6 %collective-permute-done.1.refs_4_ = bf16[96,512]{1,0:T(8,128)(2,1)S(1)} collective-permute-done((bf16[96,512]{1,0:T(8,128)(2,1)}, bf16[96,512]{1,0:T(8,128)(2,1)S(1)}, u32[]{:S(2)}, u32[]{:S(2)}) %collective-permute-start.1) | collective-permute-done | bytes 98336 | tf_op jit(solution)/shard_map/ppermute | solution.py:270
  19.2 2.3 %collective-permute-done.refs_3_ = bf16[96,512]{1,0:T(8,128)(2,1)S(1)} collective-permute-done((bf16[96,512]{1,0:T(8,128)(2,1)}, bf16[96,512]{1,0:T(8,128)(2,1)S(1)}, u32[]{:S(2)}, u32[]{:S(2)}) %collective-permute-start) | collective-permute-done | bytes 98336 | tf_op jit(solution)/shard_map/ppermute | solution.py:270
  21.5 1.0 collective-permute-done.2.refs_5_
  22.4 1.7 %all-to-all-done.refs_7_ = bf16[16,32,256]{2,1,0:T(8,128)(2,1)S(1)} async-done(((bf16[16,32,256]{2,1,0:T(8,128)(2,1)}), bf16[16,32,256]{2,1,0:T(8,128)(2,1)S(1)}, u32[]{:S(2)}, u32[]{:S(2)}) %all-to-all-start) | async-done | bytes 262176 | tf_op jit(solution)/shard_map/all_to_all | solution.py:61
  24.1 0.0 copy-start.1
  24.1 0.0 copy-start.2
  24.1 10.9 %shard_map.77 = (bf16[16,2048,256]{2,1,0:T(8,128)(2,1)S(1)}, f32[16,32,128]{2,1,0:T(8,128)S(1)}) custom-call(s32[1]{0:T(128)} %bitcast.refs_0_.refs_1_, s32[1]{0:T(128)} %bitcast.refs_0_.refs_1_, bf16[96,512]{1,0:T(8,128)(2,1)} %refs_2_.1, bf16[96,512]{1,0:T(8,128)(2,1)S(1)} %collective-permute-done.refs_3_, ...), custom_call_target="tpu_custom_call" | custom-call | flops 2684354560 | bytes 16777216 | tf_op jit(solution)/shard_map/pallas_call | solution.py:147
  35.1 14.0 %all_to_all.25.parts_ref = f32[16,32,128]{2,1,0:T(8,128)S(1)} all-to-all(f32[16,32,128]{2,1,0:T(8,128)S(1)} %get-tuple-element.7), channel_id=1, replica_groups=mesh['yh'=2,'zh'=2,'zm'=2,'zl'=2,'x'=4,'yl'=2,'c'=2] {'x','yl','c'}, dimensions={0} | all-to-all | bytes 524288 | tf_op jit(solution)/shard_map/all_to_all | solution.py:61
  49.1 9.0 %all_to_all.26.rows_ref = bf16[16,32,128]{2,1,0:T(8,128)(2,1)S(1)} all-to-all(bf16[16,32,128]{2,1,0:T(8,128)(2,1)S(1)} %shard_map.78), channel_id=1, replica_groups=mesh['yh'=2,'zh'=2,'zm'=2,'zl'=2,'x'=4,'yl'=2,'c'=2] {'x','yl','c'}, dimensions={0} | all-to-all | bytes 262144 | tf_op jit(solution)/shard_map/all_to_all | solution.py:61
  58.1 3.1 %shard_map.79 = f32[16,72,128]{2,1,0:T(8,128)S(1)} custom-call(bf16[16,32,128]{2,1,0:T(8,128)(2,1)S(1)} %all_to_all.26.rows_ref, bf16[16,2048,256]{2,1,0:T(8,128)(2,1)S(1)} %get-tuple-element.8.k_ref), custom_call_target="tpu_custom_call" | custom-call | flops 536870912 | bytes 16777216 | tf_op jit(solution)/shard_map/pallas_call | solution.py:197
  61.3 17.0 %all_to_all.27 = f16[16,72,128]{2,1,0:T(8,128)(2,1)S(1)} all-to-all(f16[16,72,128]{2,1,0:T(8,128)(2,1)S(1)} %convert_element_type.6), channel_id=1, replica_groups=mesh['yh'=2,'zh'=2,'zm'=2,'zl'=2,'x'=4,'yl'=2,'c'=2] {'yh','zh','zm','zl'}, dimensions={0} | all-to-all | bytes 589824 | tf_op jit(solution)/shard_map/all_to_all | solution.py:289
  78.3 0.0 copy-done.1
  78.3 0.0 copy-done.2
  78.3 0.5 shard_map.80
  78.9 20.9 %all_to_all.28 = f32[256,1,128]{2,1,0:T(1,128)S(1)} all-to-all(f32[256,1,128]{2,1,0:T(1,128)S(1)} %bitcast.6), channel_id=1, replica_groups=mesh['yh'=2,'zh'=2,'zm'=2,'zl'=2,'x'=4,'yl'=2,'c'=2] {'yh','zh','zm','zl..., dimensions={0} | all-to-all | bytes 262144 | tf_op jit(solution)/shard_map/all_to_all | solution.py:291
  99.7 0.0 copy-done.3
  99.7 0.9 shard_map.81
  (4 shorter events, 0.1 us)
Async XLA Ops:
  0.6 0.8 copy-start
  2.1 22.0 %all-to-all-start = ((bf16[16,32,256]{2,1,0:T(8,128)(2,1)}), bf16[16,32,256]{2,1,0:T(8,128)(2,1)S(1)}, u32[]{:S(2)}, u32[]{:S(2)}) async-start(bf16[16,32,256]{2,1,0:T(8,128)(2,1)} %shard_map.76), calls=%async_computation | async-start | bytes 524288 | tf_op jit(solution)/shard_map/all_to_all | solution.py:61
  13.9 5.3 %collective-permute-start.1 = (bf16[96,512]{1,0:T(8,128)(2,1)}, bf16[96,512]{1,0:T(8,128)(2,1)S(1)}, u32[]{:S(2)}, u32[]{:S(2)}) collective-permute-start(bf16[96,512]{1,0:T(8,128)(2,1)} %refs_2_.1), channel_id=1, source_target_pairs={{0,8},{4,12},{8,0},{12,4},{1,9},{5,13},{9,1},{13,5},{2,10},{6,14},... | collective-permute-start | bytes 294920 | tf_op jit(solution)/shard_map/ppermute | solution.py:270
  16.7 4.8 %collective-permute-start = (bf16[96,512]{1,0:T(8,128)(2,1)}, bf16[96,512]{1,0:T(8,128)(2,1)S(1)}, u32[]{:S(2)}, u32[]{:S(2)}) collective-permute-start(bf16[96,512]{1,0:T(8,128)(2,1)} %refs_2_.1), channel_id=1, source_target_pairs={{0,4},{4,0},{8,12},{12,8},{1,5},{5,1},{9,13},{13,9},{2,6},{6,2},{1... | collective-permute-start | bytes 294920 | tf_op jit(solution)/shard_map/ppermute | solution.py:270
  17.0 5.4 %collective-permute-start.2 = (bf16[96,512]{1,0:T(8,128)(2,1)}, bf16[96,512]{1,0:T(8,128)(2,1)S(1)}, u32[]{:S(2)}, u32[]{:S(2)}) collective-permute-start(bf16[96,512]{1,0:T(8,128)(2,1)} %refs_2_.1), channel_id=1, source_target_pairs={{0,12},{4,8},{8,4},{12,0},{1,13},{5,9},{9,5},{13,1},{2,14},{6,10},... | collective-permute-start | bytes 294920 | tf_op jit(solution)/shard_map/ppermute | solution.py:270
  24.1 54.2 %copy-start.1 = (f32[32,256]{1,0:T(8,128)S(1)}, f32[32,256]{1,0:T(8,128)}, u32[]{:S(2)}) copy-start(f32[32,256]{1,0:T(8,128)} %d_ref.5) | copy-start | bytes 98308
  24.1 54.2 %copy-start.2 = (f32[32,256]{1,0:T(8,128)S(1)}, f32[32,256]{1,0:T(8,128)}, u32[]{:S(2)}) copy-start(f32[32,256]{1,0:T(8,128)} %r_ref.3) | copy-start | bytes 98308
  24.1 75.6 %copy-start.3 = (f32[32,256]{1,0:T(8,128)S(1)}, f32[32,256]{1,0:T(8,128)}, u32[]{:S(2)}) copy-start(f32[32,256]{1,0:T(8,128)} %coeffs_ref.1) | copy-start | bytes 98308

commit v4 on v3

v4 whole, which is shorter than its diff:
```python
import functools

import jax
import jax.numpy as jnp
from jax import lax
from jax.experimental import pallas as pl
from jax.experimental.pallas import tpu as pltpu
from jax.sharding import Mesh, PartitionSpec as P

AXES = ("yh", "z", "x", "yl", "c")
SIZES = (2, 8, 4, 2, 2)
EP = ("yh", "z", "x")
CTR = ("yl", "c")
SPLIT = ("yh", "z")
ROWS = ("x", "yl", "c")
N_SPLIT, N_X, N_ROWS = 16, 4, 16

F = 96
DEPTH = 128
TGT = 32
PIECE = 256
ROWPIECE = 128
OWN = 512
PER = OWN // ROWPIECE
N_EP = N_X * OWN
EARLY = 2 * OWN
SHARP = 3.0 / F
F32 = jnp.float32
BF16 = jnp.bfloat16
F16 = jnp.float16
IN_VMEM = pl.BlockSpec(memory_space=pltpu.VMEM)
IN_SMEM = pl.BlockSpec(memory_space=pltpu.SMEM)
ANYWHERE = pl.BlockSpec(memory_space=pl.ANY)


def params(mib):
    return pltpu.CompilerParams(vmem_limit_bytes=mib * 1024 * 1024)


def here(x):
    return pltpu.with_memory_space_constraint(x, pltpu.VMEM)


def in_hbm(x):
    return pltpu.with_memory_space_constraint(x, pltpu.HBM)


def exchange(x, axes):
    return here(lax.all_to_all(here(x), axes, 0, 0, tiled=False))


def three(v):
    hi = v.astype(BF16).astype(F32)
    mid = (v - hi).astype(BF16).astype(F32)
    return hi, mid, v - hi - mid


def extra_rows(norm_parts, first, width):
    row = lax.broadcasted_iota(jnp.int32, (DEPTH - F, width), 0)
    out = jnp.where(row < 6, 1.0, 0.0).astype(F32)
    for k, part in enumerate(norm_parts):
        out = jnp.where(row == first + k, part, out)
    return out


def copies_kernel(d_ref, out_ref, mine, sem):
    load = pltpu.make_async_copy(d_ref, mine, sem)
    load.start()
    load.wait()
    half = mine[...].astype(BF16)
    for i in range(N_SPLIT):
        out_ref[i] = half


def copies(direction):
    return pl.pallas_call(
        copies_kernel,
        in_specs=[ANYWHERE],
        out_specs=IN_VMEM,
        out_shape=pltpu.VMEM((N_SPLIT, TGT, PIECE), BF16),
        scratch_shapes=[pltpu.VMEM((TGT, PIECE), F32), pltpu.SemaphoreType.DMA],
        compiler_params=params(4),
    )(in_hbm(direction))


def left_block(e):
    e = e.astype(F32)
    norm = jnp.sum(e * e, axis=0, keepdims=True)
    tall = jnp.concatenate([e * (2.0 * SHARP), extra_rows(three(-SHARP * norm), 0, OWN)], axis=0)
    return tall.T.astype(BF16)


def tile(left, right):
    return jnp.exp(jnp.dot(left, right, preferred_element_type=F32)).astype(BF16)


def early_kernel(place_ref, own_ref, next_ref, cen_ref, k_ref, right_ref, left, own, cens, ready, cen_sems, own_sem,
                 out_sems):
    def fetch(i):
        start = pl.multiple_of((place_ref[0] + i * N_X) * PIECE, PIECE)
        return pltpu.make_async_copy(cen_ref.at[:, pl.ds(start, PIECE)], cens.at[i], cen_sems.at[i])

    def store(i):
        return pltpu.make_async_copy(ready.at[i], k_ref.at[i], out_sems.at[i])

    mine = pltpu.make_async_copy(own_ref, own, own_sem)
    mine.start()
    for i in range(N_SPLIT):
        fetch(i).start()
    left[OWN:, :] = left_block(next_ref[...])
    mine.wait()
    left[:OWN, :] = left_block(own[...])
    for i in range(N_SPLIT):
        fetch(i).wait()
    for i in range(N_SPLIT):
        c = cens[i].astype(F32)
        norm = jnp.sum(c * c, axis=0, keepdims=True)
        right = jnp.concatenate([cens[i], extra_rows(three(-SHARP * norm), 3, PIECE).astype(BF16)], axis=0)
        right_ref[i] = right
        for r in range(0, EARLY, 256):
            ready[i, r:r + 256, :] = tile(left[r:r + 256, :], right)
        store(i).start()
    for i in range(N_SPLIT):
        store(i).wait()


def early_tiles(place, own, near, centers):
    return pl.pallas_call(
        early_kernel,
        in_specs=[IN_SMEM, ANYWHERE, IN_VMEM, ANYWHERE],
        out_specs=(ANYWHERE, IN_VMEM),
        out_shape=(
            pltpu.HBM((N_SPLIT, EARLY, PIECE), BF16),
            jax.ShapeDtypeStruct((N_SPLIT, DEPTH, PIECE), BF16),
        ),
        scratch_shapes=[
            pltpu.VMEM((EARLY, DEPTH), BF16),
            pltpu.VMEM((F, OWN), BF16),
            pltpu.VMEM((N_SPLIT, F, PIECE), BF16),
            pltpu.VMEM((N_SPLIT, EARLY, PIECE), BF16),
            pltpu.SemaphoreType.DMA((N_SPLIT,)),
            pltpu.SemaphoreType.DMA,
            pltpu.SemaphoreType.DMA((N_SPLIT,)),
        ],
        compiler_params=params(20),
        cost_estimate=pl.CostEstimate(flops=10 ** 11, bytes_accessed=2 ** 23, transcendentals=2 ** 22),
    )(place, in_hbm(own), near, in_hbm(centers))


def late_kernel(x_ref, p2_ref, p3_ref, right_ref, early_ref, d_ref, k_ref, out_ref, left, sem):
    load = pltpu.make_async_copy(early_ref, k_ref.at[:, pl.ds(0, EARLY), :], sem)
    load.start()
    for m, ref in enumerate((p2_ref, p3_ref)):
        left[m * OWN:(m + 1) * OWN, :] = left_block(ref[...])
    for i in range(N_SPLIT):
        for r in range(0, N_EP - EARLY, 256):
            k_ref[i, EARLY + r:EARLY + r + 256, :] = tile(left[r:r + 256, :], right_ref[i])
    for m in (2, 3, 0, 1):
        if m == 0:
            load.wait()
        total = None
        for i in range(N_SPLIT):
            part = lax.dot_general(
                k_ref[i, m * OWN:(m + 1) * OWN, :], d_ref[i], (((1,), (1,)), ((), ())), preferred_element_type=F32
            )
            total = part if total is None else total + part
        total = total.T
        for q in range(PER):
            out_ref[(x_ref[0] ^ m) * PER + q] = total[:, q * ROWPIECE:(q + 1) * ROWPIECE]


def tiles_and_rows(x, far, right, early, dirs):
    return pl.pallas_call(
        late_kernel,
        in_specs=[IN_SMEM] + [IN_VMEM] * 3 + [ANYWHERE, IN_VMEM],
        out_specs=(IN_VMEM,) * 2,
        out_shape=(
            pltpu.VMEM((N_SPLIT, N_EP, PIECE), BF16),
            pltpu.VMEM((N_ROWS, TGT, ROWPIECE), F32),
        ),
        scratch_shapes=[pltpu.VMEM((N_EP - EARLY, DEPTH), BF16), pltpu.SemaphoreType.DMA],
        compiler_params=params(16),
        cost_estimate=pl.CostEstimate(
            flops=2 * (DEPTH + TGT) * 2 ** 23, bytes_accessed=2 ** 24, transcendentals=2 ** 23
        ),
    )(x, *far, right, in_hbm(early), dirs)


def spread_kernel(parts_ref, out_ref):
    half = jnp.sum(parts_ref[...], axis=0).astype(BF16)
    for j in range(N_ROWS):
        out_ref[j] = half


def spread(parts):
    return pl.pallas_call(
        spread_kernel, out_shape=pltpu.VMEM((N_ROWS, TGT, ROWPIECE), BF16), compiler_params=params(4)
    )(parts)


MESSAGE = 72
HALF = PIECE // 2


def column_kernel(x_ref, rows_ref, k_ref, out_ref, half):
    for m in range(N_X):
        for q in range(PER):
            c = m * OWN + q * ROWPIECE
            half[:, c:c + ROWPIECE] = rows_ref[(x_ref[0] ^ m) * PER + q]
    sums = [jnp.dot(half[...], k_ref[i], preferred_element_type=F32) for i in range(N_SPLIT)]
    top = functools.reduce(jnp.maximum, [jnp.abs(v) for v in sums])
    top = jnp.max(jnp.maximum(top[:, :HALF], top[:, HALF:]), axis=1, keepdims=True)
    power = jnp.ceil(jnp.log2(jnp.maximum(jnp.broadcast_to(top, (TGT, HALF)), 1e-30)))
    scale = jnp.exp2(15.0 - power)
    line = jnp.concatenate([power] * (HALF // TGT), axis=0).T[:MESSAGE - 2 * TGT]
    for i in range(N_SPLIT):
        out_ref[i, :TGT, :] = sums[i][:, :HALF] * scale
        out_ref[i, TGT:2 * TGT, :] = sums[i][:, HALF:] * scale
        out_ref[i, 2 * TGT:, :] = line


def column_sums(x, rows, kmat):
    return pl.pallas_call(
        column_kernel,
        in_specs=[IN_SMEM] + [IN_VMEM] * 2,
        out_specs=IN_VMEM,
        out_shape=jax.ShapeDtypeStruct((N_SPLIT, MESSAGE, HALF), F32),
        scratch_shapes=[pltpu.VMEM((TGT, N_EP), BF16)],
        compiler_params=params(8),
        cost_estimate=pl.CostEstimate(flops=2 * TGT * 2 ** 23, bytes_accessed=2 ** 24, transcendentals=0),
    )(x, rows, here(kmat))


def gathered(parts_ref):
    low = high = 0.0
    for i in range(N_SPLIT):
        power = jnp.broadcast_to(parts_ref[i, 2 * TGT:2 * TGT + 1, :], (HALF, HALF)).T[:TGT]
        back = jnp.exp2(power - 15.0)
        low = low + parts_ref[i, :TGT, :] * back
        high = high + parts_ref[i, TGT:2 * TGT, :] * back
    return jnp.concatenate([low, high], axis=1)


def lane_sums(v):
    return jnp.broadcast_to(jnp.sum(v, axis=1, keepdims=True), (TGT, 128))


def wide(v):
    return jnp.concatenate([v, v], axis=1)


def apply_kernel(parts_ref, r_ref, d_ref, applied_ref, sums_ref):
    r, d = r_ref[...], d_ref[...]
    a = gathered(parts_ref) + 1.0 * d
    applied_ref[...] = a
    aa = lane_sums(a * a)
    fit = jnp.where(aa > 0.0, lane_sums(r * a) / jnp.where(aa > 0.0, aa, 1.0), 0.0)
    rest = r - wide(fit) * a
    cols = jnp.concatenate([lane_sums(rest * rest), fit, aa, lane_sums(d * a)], axis=0)
    sums_ref[...] = jnp.broadcast_to(cols.T[:1], sums_ref.shape)


def apply_and_sum(parts, residual, direction):
    return pl.pallas_call(
        apply_kernel,
        out_shape=(pltpu.VMEM((TGT, PIECE), F32), jax.ShapeDtypeStruct((256, 4 * TGT), F32)),
        compiler_params=params(4),
    )(parts, residual, direction)


def step_kernel(sums_ref, coeffs_ref, r_ref, d_ref, a_ref, co_ref, ro_ref, do_ref):
    rest, fit, aa, da = (sums_ref[:, k * TGT:(k + 1) * TGT] for k in range(4))
    old = jnp.sum(rest + fit * (fit * aa), axis=0, keepdims=True)
    step = old / jnp.sum(da, axis=0, keepdims=True)
    off = step - fit
    new = jnp.sum(rest + off * (off * aa), axis=0, keepdims=True)
    step = wide(jnp.broadcast_to(step, (128, TGT)).T)
    beta = wide(jnp.broadcast_to(new / old, (128, TGT)).T)
    d = d_ref[...]
    co_ref[...] = coeffs_ref[...] + step * d
    res = r_ref[...] - step * a_ref[...]
    ro_ref[...] = res
    do_ref[...] = res + beta * d


def step_and_update(sums, coeffs, residual, direction, applied):
    return pl.pallas_call(
        step_kernel,
        out_shape=(jax.ShapeDtypeStruct((TGT, PIECE), F32),) * 3,
        compiler_params=params(4),
    )(sums, coeffs, residual, direction, here(applied))


def from_x(v, m):
    return lax.ppermute(v, "x", [(k, k ^ m) for k in range(N_X)])


def shards(episodes, centers, coeffs, residual, direction):
    x = lax.axis_index("x").reshape(1)
    near = from_x(episodes, 1)
    far = from_x(near, 3), from_x(near, 2)
    dirs = exchange(copies(direction), SPLIT)
    early, right = early_tiles(x, episodes, near, centers)
    kmat, row_parts = tiles_and_rows(x, far, right, early, dirs)
    row_parts = exchange(row_parts, ROWS)
    rows = exchange(spread(row_parts), ROWS)
    parts = column_sums(x, rows, kmat).astype(F16)
    parts = lax.all_to_all(parts, SPLIT, 0, 0, tiled=False).astype(F32)
    applied, sums = apply_and_sum(parts, residual, direction)
    sums = lax.all_to_all(sums.reshape(256, 1, 4 * TGT), AXES, 0, 0, tiled=False).reshape(256, 4 * TGT)
    return step_and_update(sums, coeffs, residual, direction, applied)


def solution(mesh):
    fine = Mesh(mesh.devices.reshape(SIZES), AXES)
    piece = P(None, CTR + EP)
    return jax.shard_map(
        shards,
        mesh=fine,
        in_specs=(P(None, EP), P(None, CTR), piece, piece, piece),
        out_specs=(piece, piece, piece),
        check_vma=False,
    )
```

time: 101 us -> 99.3 us (0.983)
  waiting for transfers between devices: 6.54 us -> 1.37 us
  Pallas kernels: 16.3 us -> 18.4 us
  blocking collectives: 60.8 us -> 62.5 us
    ppermute x3, waiting for transfers between devices: 4.85 us -> 0.14 us  [from_x(): return lax.ppermute(v, 'x', [(k, k ^ m) for k in range(N_X)])]
    pallas_call x3 -> x4, Pallas kernels: 14.8 us -> 16.9 us  [the longest x1 7.01 us: tiles_and_rows(): pl.pallas_call(late_kernel, in_specs=[IN_SMEM] + [IN_VMEM] * 3 + [ANYWHER...]
    all_to_all x1, blocking collectives: 17 us -> 18.2 us  [shards(): parts = lax.all_to_all(parts, SPLIT, 0, 0, tiled=False).astype(F32)]
    ppermute x3, starting transfers between devices: 3.69 us -> 4.86 us  [from_x(): return lax.ppermute(v, 'x', [(k, k ^ m) for k in range(N_X)])]
  transfers between devices with their start and end apart: 4 -> 4, of which waited for: 4 -> 2; matrix products, arithmetic and copies ran while one was open for 0% -> 0% of each run, Pallas kernels for 0% -> 7%
where the time goes in v4:
time: 99.3 us; the launch traced here: 98.9 us
  blocking collectives  62.5 us (63%)
  Pallas kernels  18.4 us (19%)
  starting transfers between devices  15.8 us (16%)
  waiting for transfers between devices  1.37 us (1%)
    all_to_all x2, blocking collectives, exchange(): return here(lax.all_to_all(here(x), axes, 0, 0, tiled=False))  23.5 us
    all_to_all x1, blocking collectives, shards(): lax.all_to_all(sums.reshape(256, 1, 4 * TGT), AXES, 0, 0, tiled=False)  20.9 us
    all_to_all x1, blocking collectives, shards(): parts = lax.all_to_all(parts, SPLIT, 0, 0, tiled=False).astype(F32)  18.2 us
    all_to_all x1, starting transfers between devices, exchange(): return here(lax.all_to_all(here(x), axes, 0, 0, tiled=False))  10.9 us
    pallas_call x1, Pallas kernels, tiles_and_rows(): pl.pallas_call(late_kernel, in_specs=[IN_SMEM] + [IN_VMEM] * 3 + [ANYWHER...  7.01 us
    pallas_call x1, Pallas kernels, early_tiles(): pl.pallas_call(early_kernel, in_specs=[IN_SMEM, ANYWHERE, IN_VMEM, ANYWHE...  5.21 us
    ppermute x3, starting transfers between devices, from_x(): return lax.ppermute(v, 'x', [(k, k ^ m) for k in range(N_X)])  4.86 us
    pallas_call x1, Pallas kernels, column_sums(): pl.pallas_call(column_kernel, in_specs=[IN_SMEM] + [IN_VMEM] * 2, out_spe...  3.11 us
  transfers between devices with their start and end apart: 4, of which 2 were waited for; matrix products, arithmetic and copies ran while one was open for 0% of the time, Pallas kernels for 7%

profile of v4, /device:TPU:1, one launch (start us, length us, event | category | flops | bytes accessed | tf_op | source)
XLA Modules:
  0.0 98.9 jit_solution(399432434424821565)
XLA Ops:
  0.6 2.1 %collective-permute-start = (bf16[96,512]{1,0:T(8,128)(2,1)}, bf16[96,512]{1,0:T(8,128)(2,1)S(1)}, u32[]{:S(2)}, u32[]{:S(2)}) collective-permute-start(bf16[96,512]{1,0:T(8,128)(2,1)} %own_ref.1), channel_id=1, source_target_pairs={{0,4},{4,0},{8,12},{12,8},{1,5},{5,1},{9,13},{13,9},{2,6},{6,2},{1... | collective-permute-start | bytes 294920 | tf_op jit(solution)/shard_map/ppermute | solution.py:295
  2.8 1.5 %shard_map.77 = bf16[16,32,256]{2,1,0:T(8,128)(2,1)} custom-call(f32[32,256]{1,0:T(8,128)} %d_ref.5), custom_call_target="tpu_custom_call" | custom-call | tf_op jit(solution)/shard_map/pallas_call | solution.py:76
  4.3 10.9 %all-to-all-start = ((bf16[16,32,256]{2,1,0:T(8,128)(2,1)}), bf16[16,32,256]{2,1,0:T(8,128)(2,1)S(1)}, u32[]{:S(2)}, u32[]{:S(2)}) async-start(bf16[16,32,256]{2,1,0:T(8,128)(2,1)} %shard_map.77), calls=%async_computation | async-start | bytes 524288 | tf_op jit(solution)/shard_map/all_to_all | solution.py:49
  15.3 0.0 collective-permute-done.next_ref
  15.3 2.5 %collective-permute-start.2 = (bf16[96,512]{1,0:T(8,128)(2,1)S(1)}, bf16[96,512]{1,0:T(8,128)(2,1)S(1)}, u32[]{:S(2)}, u32[]{:S(2)}) collective-permute-start(bf16[96,512]{1,0:T(8,128)(2,1)S(1)} %collective-permute-done.next_ref), channel_id=1, source_target_pairs={{0,8},{4,12},{8,0},{12,4},{1,9},{5,13},{9,1},{13,5},{2,10},{6,14},... | collective-permute-start | bytes 294920 | tf_op jit(solution)/shard_map/ppermute | solution.py:295
  17.8 0.2 collective-permute-start.1
  18.0 5.2 %shard_map.76 = (bf16[16,1024,256]{2,1,0:T(8,128)(2,1)}, bf16[16,128,256]{2,1,0:T(8,128)(2,1)S(1)}) custom-call(s32[1]{0:T(128)} %bitcast.place_ref.x_ref, bf16[96,512]{1,0:T(8,128)(2,1)} %own_ref.1, bf16[96,512]{1,0:T(8,128)(2,1)S(1)} %collective-permute-done.next_ref, bf16[96,16384]{1,0:T(8,128)(2,1)} %cen_ref.1), custom_call_target="tpu_custom_call" | custom-call | flops 99999997952 | bytes 8388608 | tf_op jit(solution)/shard_map/pallas_call | solution.py:128
  23.2 0.0 collective-permute-done.2.p3_ref
  23.2 0.1 collective-permute-done.1.p2_ref
  23.4 1.2 %all-to-all-done.d_ref = bf16[16,32,256]{2,1,0:T(8,128)(2,1)S(1)} async-done(((bf16[16,32,256]{2,1,0:T(8,128)(2,1)}), bf16[16,32,256]{2,1,0:T(8,128)(2,1)S(1)}, u32[]{:S(2)}, u32[]{:S(2)}) %all-to-all-start) | async-done | bytes 262176 | tf_op jit(solution)/shard_map/all_to_all | solution.py:49
  24.6 7.0 %shard_map.78 = (bf16[16,2048,256]{2,1,0:T(8,128)(2,1)S(1)}, f32[16,32,128]{2,1,0:T(8,128)S(1)}) custom-call(s32[1]{0:T(128)} %bitcast.place_ref.x_ref, bf16[96,512]{1,0:T(8,128)(2,1)S(1)} %collective-permute-done.1.p2_ref, bf16[96,512]{1,0:T(8,128)(2,1)S(1)} %collective-permute-done.2.p3_ref, bf16[16,128,256]{2,1,0:T(8,128)(2,1)S(1)} %get-tuple-element.9.right_ref, ...), custom_call_target="tpu_custom_call" | custom-call | flops 2684354560 | bytes 16777216 | tf_op jit(solution)/shard_map/pallas_call | solution.py:173
  31.6 14.4 %all_to_all.25.parts_ref = f32[16,32,128]{2,1,0:T(8,128)S(1)} all-to-all(f32[16,32,128]{2,1,0:T(8,128)S(1)} %get-tuple-element.11), channel_id=1, replica_groups=mesh['yh'=2,'z'=8,'x'=4,'yl'=2,'c'=2] {'x','yl','c'}, dimensions={0} | all-to-all | bytes 524288 | tf_op jit(solution)/shard_map/all_to_all | solution.py:49
  46.1 9.0 %all_to_all.26.rows_ref = bf16[16,32,128]{2,1,0:T(8,128)(2,1)S(1)} all-to-all(bf16[16,32,128]{2,1,0:T(8,128)(2,1)S(1)} %shard_map.79), channel_id=1, replica_groups=mesh['yh'=2,'z'=8,'x'=4,'yl'=2,'c'=2] {'x','yl','c'}, dimensions={0} | all-to-all | bytes 262144 | tf_op jit(solution)/shard_map/all_to_all | solution.py:49
  55.1 0.0 copy-start
  55.1 0.0 copy-start.1
  55.1 0.0 copy-start.2
  55.1 3.1 %shard_map.80 = f32[16,72,128]{2,1,0:T(8,128)S(1)} custom-call(s32[1]{0:T(128)} %bitcast.place_ref.x_ref, bf16[16,32,128]{2,1,0:T(8,128)(2,1)S(1)} %all_to_all.26.rows_ref, bf16[16,2048,256]{2,1,0:T(8,128)(2,1)S(1)} %get-tuple-element.12.k_ref), custom_call_target="tpu_custom_call" | custom-call | flops 536870912 | bytes 16777216 | tf_op jit(solution)/shard_map/pallas_call | solution.py:223
  58.3 18.2 %all_to_all.27 = f16[16,72,128]{2,1,0:T(8,128)(2,1)S(1)} all-to-all(f16[16,72,128]{2,1,0:T(8,128)(2,1)S(1)} %convert_element_type.6), channel_id=1, replica_groups=mesh['yh'=2,'z'=8,'x'=4,'yl'=2,'c'=2] {'yh','z'}, dimensions={0} | all-to-all | bytes 589824 | tf_op jit(solution)/shard_map/all_to_all | solution.py:308
  76.5 0.0 copy-done
  76.5 0.0 copy-done.1
  76.5 0.5 shard_map.81
  77.1 20.9 %all_to_all.28 = f32[256,1,128]{2,1,0:T(1,128)S(1)} all-to-all(f32[256,1,128]{2,1,0:T(1,128)S(1)} %bitcast.6), channel_id=1, replica_groups=mesh['yh'=2,'z'=8,'x'=4,'yl'=2,'c'=2] {'yh','z','x','yl','c'}, dimensions={0} | all-to-all | bytes 262144 | tf_op jit(solution)/shard_map/all_to_all | solution.py:310
  97.9 0.0 copy-done.2
  97.9 0.9 shard_map.82
  (3 shorter events, 0.1 us)
Async XLA Ops:
  0.6 14.6 %collective-permute-start = (bf16[96,512]{1,0:T(8,128)(2,1)}, bf16[96,512]{1,0:T(8,128)(2,1)S(1)}, u32[]{:S(2)}, u32[]{:S(2)}) collective-permute-start(bf16[96,512]{1,0:T(8,128)(2,1)} %own_ref.1), channel_id=1, source_target_pairs={{0,4},{4,0},{8,12},{12,8},{1,5},{5,1},{9,13},{13,9},{2,6},{6,2},{1... | collective-permute-start | bytes 294920 | tf_op jit(solution)/shard_map/ppermute | solution.py:295
  4.3 20.3 %all-to-all-start = ((bf16[16,32,256]{2,1,0:T(8,128)(2,1)}), bf16[16,32,256]{2,1,0:T(8,128)(2,1)S(1)}, u32[]{:S(2)}, u32[]{:S(2)}) async-start(bf16[16,32,256]{2,1,0:T(8,128)(2,1)} %shard_map.77), calls=%async_computation | async-start | bytes 524288 | tf_op jit(solution)/shard_map/all_to_all | solution.py:49
  15.3 8.0 %collective-permute-start.2 = (bf16[96,512]{1,0:T(8,128)(2,1)S(1)}, bf16[96,512]{1,0:T(8,128)(2,1)S(1)}, u32[]{:S(2)}, u32[]{:S(2)}) collective-permute-start(bf16[96,512]{1,0:T(8,128)(2,1)S(1)} %collective-permute-done.next_ref), channel_id=1, source_target_pairs={{0,8},{4,12},{8,0},{12,4},{1,9},{5,13},{9,1},{13,5},{2,10},{6,14},... | collective-permute-start | bytes 294920 | tf_op jit(solution)/shard_map/ppermute | solution.py:295
  17.8 5.6 %collective-permute-start.1 = (bf16[96,512]{1,0:T(8,128)(2,1)S(1)}, bf16[96,512]{1,0:T(8,128)(2,1)S(1)}, u32[]{:S(2)}, u32[]{:S(2)}) collective-permute-start(bf16[96,512]{1,0:T(8,128)(2,1)S(1)} %collective-permute-done.next_ref), channel_id=1, source_target_pairs={{0,12},{4,8},{8,4},{12,0},{1,13},{5,9},{9,5},{13,1},{2,14},{6,10},... | collective-permute-start | bytes 294920 | tf_op jit(solution)/shard_map/ppermute | solution.py:295
  55.1 21.4 %copy-start = (f32[32,256]{1,0:T(8,128)S(1)}, f32[32,256]{1,0:T(8,128)}, u32[]{:S(2)}) copy-start(f32[32,256]{1,0:T(8,128)} %d_ref.5) | copy-start | bytes 98308
  55.1 21.4 %copy-start.1 = (f32[32,256]{1,0:T(8,128)S(1)}, f32[32,256]{1,0:T(8,128)}, u32[]{:S(2)}) copy-start(f32[32,256]{1,0:T(8,128)} %r_ref.3) | copy-start | bytes 98308
  55.1 42.8 %copy-start.2 = (f32[32,256]{1,0:T(8,128)S(1)}, f32[32,256]{1,0:T(8,128)}, u32[]{:S(2)}) copy-start(f32[32,256]{1,0:T(8,128)} %coeffs_ref.1) | copy-start | bytes 98308

commit v5 on v4

--- a/solution.py
+++ b/solution.py
@@ -63,24 +63,34 @@
     return out
 
 
-def copies_kernel(d_ref, out_ref, mine, sem):
-    load = pltpu.make_async_copy(d_ref, mine, sem)
-    load.start()
-    load.wait()
+def first_kernel(place_ref, d_ref, e_ref, cen_ref, out_ref, own_ref, cens_ref, mine, sems):
+    loads = [pltpu.make_async_copy(d_ref, mine, sems.at[0]), pltpu.make_async_copy(e_ref, own_ref, sems.at[1])]
+    for i in range(N_SPLIT):
+        start = pl.multiple_of((place_ref[0] + i * N_X) * PIECE, PIECE)
+        loads.append(pltpu.make_async_copy(cen_ref.at[:, pl.ds(start, PIECE)], cens_ref.at[i], sems.at[2 + i]))
+    for load in loads:
+        load.start()
+    loads[0].wait()
     half = mine[...].astype(BF16)
     for i in range(N_SPLIT):
         out_ref[i] = half
-
-
-def copies(direction):
-    return pl.pallas_call(
-        copies_kernel,
-        in_specs=[ANYWHERE],
-        out_specs=IN_VMEM,
-        out_shape=pltpu.VMEM((N_SPLIT, TGT, PIECE), BF16),
-        scratch_shapes=[pltpu.VMEM((TGT, PIECE), F32), pltpu.SemaphoreType.DMA],
+    for load in loads[1:]:
+        load.wait()
+
+
+def first_copies(place, direction, episodes, centers):
+    return pl.pallas_call(
+        first_kernel,
+        in_specs=[IN_SMEM] + [ANYWHERE] * 3,
+        out_specs=(IN_VMEM,) * 3,
+        out_shape=(
+            pltpu.VMEM((N_SPLIT, TGT, PIECE), BF16),
+            pltpu.VMEM((F, OWN), BF16),
+            pltpu.VMEM((N_SPLIT, F, PIECE), BF16),
+        ),
+        scratch_shapes=[pltpu.VMEM((TGT, PIECE), F32), pltpu.SemaphoreType.DMA((2 + N_SPLIT,))],
         compiler_params=params(4),
-    )(in_hbm(direction))
+    )(place, in_hbm(direction), in_hbm(episodes), in_hbm(centers))
 
 
 def left_block(e):
@@ -94,24 +104,12 @@
     return jnp.exp(jnp.dot(left, right, preferred_element_type=F32)).astype(BF16)
 
 
-def early_kernel(place_ref, own_ref, next_ref, cen_ref, k_ref, right_ref, left, own, cens, ready, cen_sems, own_sem,
-                 out_sems):
-    def fetch(i):
-        start = pl.multiple_of((place_ref[0] + i * N_X) * PIECE, PIECE)
-        return pltpu.make_async_copy(cen_ref.at[:, pl.ds(start, PIECE)], cens.at[i], cen_sems.at[i])
-
+def early_kernel(own_ref, next_ref, cens, k_ref, right_ref, left, ready, out_sems):
     def store(i):
         return pltpu.make_async_copy(ready.at[i], k_ref.at[i], out_sems.at[i])
 
-    mine = pltpu.make_async_copy(own_ref, own, own_sem)
-    mine.start()
-    for i in range(N_SPLIT):
-        fetch(i).start()
+    left[:OWN, :] = left_block(own_ref[...])
     left[OWN:, :] = left_block(next_ref[...])
-    mine.wait()
-    left[:OWN, :] = left_block(own[...])
-    for i in range(N_SPLIT):
-        fetch(i).wait()
     for i in range(N_SPLIT):
         c = cens[i].astype(F32)
         norm = jnp.sum(c * c, axis=0, keepdims=True)
@@ -124,10 +122,10 @@
         store(i).wait()
 
 
-def early_tiles(place, own, near, centers):
+def early_tiles(own, near, cens):
     return pl.pallas_call(
         early_kernel,
-        in_specs=[IN_SMEM, ANYWHERE, IN_VMEM, ANYWHERE],
+        in_specs=[IN_VMEM] * 3,
         out_specs=(ANYWHERE, IN_VMEM),
         out_shape=(
             pltpu.HBM((N_SPLIT, EARLY, PIECE), BF16),
@@ -135,16 +133,12 @@
         ),
         scratch_shapes=[
             pltpu.VMEM((EARLY, DEPTH), BF16),
-            pltpu.VMEM((F, OWN), BF16),
-            pltpu.VMEM((N_SPLIT, F, PIECE), BF16),
             pltpu.VMEM((N_SPLIT, EARLY, PIECE), BF16),
-            pltpu.SemaphoreType.DMA((N_SPLIT,)),
-            pltpu.SemaphoreType.DMA,
             pltpu.SemaphoreType.DMA((N_SPLIT,)),
         ],
         compiler_params=params(20),
         cost_estimate=pl.CostEstimate(flops=10 ** 11, bytes_accessed=2 ** 23, transcendentals=2 ** 22),
-    )(place, in_hbm(own), near, in_hbm(centers))
+    )(own, near, cens)
 
 
 def late_kernel(x_ref, p2_ref, p3_ref, right_ref, early_ref, d_ref, k_ref, out_ref, left, sem):
@@ -297,10 +291,11 @@
 
 def shards(episodes, centers, coeffs, residual, direction):
     x = lax.axis_index("x").reshape(1)
-    near = from_x(episodes, 1)
+    dirs, own, cens = first_copies(x, direction, episodes, centers)
+    near = from_x(own, 1)
     far = from_x(near, 3), from_x(near, 2)
-    dirs = exchange(copies(direction), SPLIT)
-    early, right = early_tiles(x, episodes, near, centers)
+    dirs = exchange(dirs, SPLIT)
+    early, right = early_tiles(own, near, cens)
     kmat, row_parts = tiles_and_rows(x, far, right, early, dirs)
     row_parts = exchange(row_parts, ROWS)
     rows = exchange(spread(row_parts), ROWS)

time: 99.3 us -> 98.2 us (0.989)
  blocking collectives: 62.5 us -> 61 us
  waiting for transfers between devices: 1.37 us -> 2.86 us
  Pallas kernels: 18.4 us -> 17.4 us
    ppermute x3, waiting for transfers between devices: 0.14 us -> 1.62 us  [from_x(): return lax.ppermute(v, 'x', [(k, k ^ m) for k in range(N_X)])]
    all_to_all x1, blocking collectives: 18.2 us -> 16.7 us  [shards(): parts = lax.all_to_all(parts, SPLIT, 0, 0, tiled=False).astype(F32)]
  transfers between devices with their start and end apart: 4 -> 4, of which waited for: 2 -> 2; matrix products, arithmetic and copies ran while one was open for 0% -> 0% of each run, Pallas kernels for 7% -> 4%
where the time goes in v5:
time: 98.2 us; the launch traced here: 97.9 us
  blocking collectives  61 us (62%)
  Pallas kernels  17.4 us (18%)
  starting transfers between devices  15.8 us (16%)
  waiting for transfers between devices  2.86 us (3%)
    all_to_all x2, blocking collectives, exchange(): return here(lax.all_to_all(here(x), axes, 0, 0, tiled=False))  23.5 us
    all_to_all x1, blocking collectives, shards(): lax.all_to_all(sums.reshape(256, 1, 4 * TGT), AXES, 0, 0, tiled=False)  20.9 us
    all_to_all x1, blocking collectives, shards(): parts = lax.all_to_all(parts, SPLIT, 0, 0, tiled=False).astype(F32)  16.7 us
    all_to_all x1, starting transfers between devices, exchange(): return here(lax.all_to_all(here(x), axes, 0, 0, tiled=False))  10.9 us
    pallas_call x1, Pallas kernels, tiles_and_rows(): pl.pallas_call(late_kernel, in_specs=[IN_SMEM] + [IN_VMEM] * 3 + [ANYWHER...  7.01 us
    ppermute x3, starting transfers between devices, from_x(): return lax.ppermute(v, 'x', [(k, k ^ m) for k in range(N_X)])  4.86 us
    pallas_call x1, Pallas kernels, early_tiles(): pl.pallas_call(early_kernel, in_specs=[IN_VMEM] * 3, out_specs=(ANYWHERE,...  3.73 us
    pallas_call x1, Pallas kernels, column_sums(): pl.pallas_call(column_kernel, in_specs=[IN_SMEM] + [IN_VMEM] * 2, out_spe...  3.12 us
  transfers between devices with their start and end apart: 4, of which 2 were waited for; matrix products, arithmetic and copies ran while one was open for 0% of the time, Pallas kernels for 4%

profile of v5, /device:TPU:1, one launch (start us, length us, event | category | flops | bytes accessed | tf_op | source)
XLA Modules:
  0.0 97.9 jit_solution(11296991344940338807)
XLA Ops:
  0.6 2.1 %shard_map.76 = (bf16[16,32,256]{2,1,0:T(8,128)(2,1)}, bf16[96,512]{1,0:T(8,128)(2,1)S(1)}, bf16[16,96,256]{2,1,0:T(8,128)(2,1)S(1)}) custom-call(s32[1]{0:T(128)} %bitcast.place_ref.x_ref, f32[32,256]{1,0:T(8,128)} %d_ref.5, bf16[96,512]{1,0:T(8,128)(2,1)} %e_ref.1, bf16[96,16384]{1,0:T(8,128)(2,1)} %cen_ref.1), custom_call_target="tpu_custom_call" | custom-call | tf_op jit(solution)/shard_map/pallas_call | solution.py:82
  2.7 2.1 %collective-permute-start = (bf16[96,512]{1,0:T(8,128)(2,1)S(1)}, bf16[96,512]{1,0:T(8,128)(2,1)S(1)}, u32[]{:S(2)}, u32[]{:S(2)}) collective-permute-start(bf16[96,512]{1,0:T(8,128)(2,1)S(1)} %get-tuple-element.12.own_ref), channel_id=1, source_target_pairs={{0,4},{4,0},{8,12},{12,8},{1,5},{5,1},{9,13},{13,9},{2,6},{6,2},{1... | collective-permute-start | bytes 294920 | tf_op jit(solution)/shard_map/ppermute | solution.py:289
  4.8 10.9 %all-to-all-start = ((bf16[16,32,256]{2,1,0:T(8,128)(2,1)}), bf16[16,32,256]{2,1,0:T(8,128)(2,1)S(1)}, u32[]{:S(2)}, u32[]{:S(2)}) async-start(bf16[16,32,256]{2,1,0:T(8,128)(2,1)} %get-tuple-element.16), calls=%async_computation | async-start | bytes 524288 | tf_op jit(solution)/shard_map/all_to_all | solution.py:49
  15.8 0.0 collective-permute-done.next_ref
  15.8 2.5 %collective-permute-start.2 = (bf16[96,512]{1,0:T(8,128)(2,1)S(1)}, bf16[96,512]{1,0:T(8,128)(2,1)S(1)}, u32[]{:S(2)}, u32[]{:S(2)}) collective-permute-start(bf16[96,512]{1,0:T(8,128)(2,1)S(1)} %collective-permute-done.next_ref), channel_id=1, source_target_pairs={{0,8},{4,12},{8,0},{12,4},{1,9},{5,13},{9,1},{13,5},{2,10},{6,14},... | collective-permute-start | bytes 294920 | tf_op jit(solution)/shard_map/ppermute | solution.py:289
  18.3 0.2 collective-permute-start.1
  18.5 3.7 %shard_map.77 = (bf16[16,1024,256]{2,1,0:T(8,128)(2,1)}, bf16[16,128,256]{2,1,0:T(8,128)(2,1)S(1)}) custom-call(bf16[96,512]{1,0:T(8,128)(2,1)S(1)} %get-tuple-element.12.own_ref, bf16[96,512]{1,0:T(8,128)(2,1)S(1)} %collective-permute-done.next_ref, bf16[16,96,256]{2,1,0:T(8,128)(2,1)S(1)} %get-tuple-element.13.cens), custom_call_target="tpu_custom_call" | custom-call | flops 99999997952 | bytes 8388608 | tf_op jit(solution)/shard_map/pallas_call | solution.py:126
  22.2 0.0 collective-permute-done.2.p3_ref
  22.2 1.6 %collective-permute-done.1.p2_ref = bf16[96,512]{1,0:T(8,128)(2,1)S(1)} collective-permute-done((bf16[96,512]{1,0:T(8,128)(2,1)S(1)}, bf16[96,512]{1,0:T(8,128)(2,1)S(1)}, u32[]{:S(2)}, u32[]{:S(2)}) %collective-permute-start.1) | collective-permute-done | bytes 98336 | tf_op jit(solution)/shard_map/ppermute | solution.py:289
  23.9 1.2 %all-to-all-done.d_ref = bf16[16,32,256]{2,1,0:T(8,128)(2,1)S(1)} async-done(((bf16[16,32,256]{2,1,0:T(8,128)(2,1)}), bf16[16,32,256]{2,1,0:T(8,128)(2,1)S(1)}, u32[]{:S(2)}, u32[]{:S(2)}) %all-to-all-start) | async-done | bytes 262176 | tf_op jit(solution)/shard_map/all_to_all | solution.py:49
  25.1 7.0 %shard_map.78 = (bf16[16,2048,256]{2,1,0:T(8,128)(2,1)S(1)}, f32[16,32,128]{2,1,0:T(8,128)S(1)}) custom-call(s32[1]{0:T(128)} %bitcast.place_ref.x_ref, bf16[96,512]{1,0:T(8,128)(2,1)S(1)} %collective-permute-done.1.p2_ref, bf16[96,512]{1,0:T(8,128)(2,1)S(1)} %collective-permute-done.2.p3_ref, bf16[16,128,256]{2,1,0:T(8,128)(2,1)S(1)} %get-tuple-element.14.right_ref, ...), custom_call_target="tpu_custom_call" | custom-call | flops 2684354560 | bytes 16777216 | tf_op jit(solution)/shard_map/pallas_call | solution.py:167
  32.1 14.4 %all_to_all.25.parts_ref = f32[16,32,128]{2,1,0:T(8,128)S(1)} all-to-all(f32[16,32,128]{2,1,0:T(8,128)S(1)} %get-tuple-element.17), channel_id=1, replica_groups=mesh['yh'=2,'z'=8,'x'=4,'yl'=2,'c'=2] {'x','yl','c'}, dimensions={0} | all-to-all | bytes 524288 | tf_op jit(solution)/shard_map/all_to_all | solution.py:49
  46.6 9.0 %all_to_all.26.rows_ref = bf16[16,32,128]{2,1,0:T(8,128)(2,1)S(1)} all-to-all(bf16[16,32,128]{2,1,0:T(8,128)(2,1)S(1)} %shard_map.79), channel_id=1, replica_groups=mesh['yh'=2,'z'=8,'x'=4,'yl'=2,'c'=2] {'x','yl','c'}, dimensions={0} | all-to-all | bytes 262144 | tf_op jit(solution)/shard_map/all_to_all | solution.py:49
  55.6 0.0 copy-start
  55.6 0.0 copy-start.1
  55.6 0.0 copy-start.2
  55.6 3.1 %shard_map.80 = f32[16,72,128]{2,1,0:T(8,128)S(1)} custom-call(s32[1]{0:T(128)} %bitcast.place_ref.x_ref, bf16[16,32,128]{2,1,0:T(8,128)(2,1)S(1)} %all_to_all.26.rows_ref, bf16[16,2048,256]{2,1,0:T(8,128)(2,1)S(1)} %get-tuple-element.18.k_ref), custom_call_target="tpu_custom_call" | custom-call | flops 536870912 | bytes 16777216 | tf_op jit(solution)/shard_map/pallas_call | solution.py:217
  58.8 16.7 %all_to_all.27 = f16[16,72,128]{2,1,0:T(8,128)(2,1)S(1)} all-to-all(f16[16,72,128]{2,1,0:T(8,128)(2,1)S(1)} %convert_element_type.6), channel_id=1, replica_groups=mesh['yh'=2,'z'=8,'x'=4,'yl'=2,'c'=2] {'yh','z'}, dimensions={0} | all-to-all | bytes 589824 | tf_op jit(solution)/shard_map/all_to_all | solution.py:303
  75.5 0.0 copy-done
  75.5 0.0 copy-done.1
  75.5 0.5 shard_map.81
  76.1 20.9 %all_to_all.28 = f32[256,1,128]{2,1,0:T(1,128)S(1)} all-to-all(f32[256,1,128]{2,1,0:T(1,128)S(1)} %bitcast.6), channel_id=1, replica_groups=mesh['yh'=2,'z'=8,'x'=4,'yl'=2,'c'=2] {'yh','z','x','yl','c'}, dimensions={0} | all-to-all | bytes 262144 | tf_op jit(solution)/shard_map/all_to_all | solution.py:305
  97.0 0.0 copy-done.2
  97.0 0.9 shard_map.82
  (3 shorter events, 0.1 us)
Async XLA Ops:
  2.7 13.1 %collective-permute-start = (bf16[96,512]{1,0:T(8,128)(2,1)S(1)}, bf16[96,512]{1,0:T(8,128)(2,1)S(1)}, u32[]{:S(2)}, u32[]{:S(2)}) collective-permute-start(bf16[96,512]{1,0:T(8,128)(2,1)S(1)} %get-tuple-element.12.own_ref), channel_id=1, source_target_pairs={{0,4},{4,0},{8,12},{12,8},{1,5},{5,1},{9,13},{13,9},{2,6},{6,2},{1... | collective-permute-start | bytes 294920 | tf_op jit(solution)/shard_map/ppermute | solution.py:289
  4.8 20.3 %all-to-all-start = ((bf16[16,32,256]{2,1,0:T(8,128)(2,1)}), bf16[16,32,256]{2,1,0:T(8,128)(2,1)S(1)}, u32[]{:S(2)}, u32[]{:S(2)}) async-start(bf16[16,32,256]{2,1,0:T(8,128)(2,1)} %get-tuple-element.16), calls=%async_computation | async-start | bytes 524288 | tf_op jit(solution)/shard_map/all_to_all | solution.py:49
  15.8 6.5 %collective-permute-start.2 = (bf16[96,512]{1,0:T(8,128)(2,1)S(1)}, bf16[96,512]{1,0:T(8,128)(2,1)S(1)}, u32[]{:S(2)}, u32[]{:S(2)}) collective-permute-start(bf16[96,512]{1,0:T(8,128)(2,1)S(1)} %collective-permute-done.next_ref), channel_id=1, source_target_pairs={{0,8},{4,12},{8,0},{12,4},{1,9},{5,13},{9,1},{13,5},{2,10},{6,14},... | collective-permute-start | bytes 294920 | tf_op jit(solution)/shard_map/ppermute | solution.py:289
  18.3 5.6 %collective-permute-start.1 = (bf16[96,512]{1,0:T(8,128)(2,1)S(1)}, bf16[96,512]{1,0:T(8,128)(2,1)S(1)}, u32[]{:S(2)}, u32[]{:S(2)}) collective-permute-start(bf16[96,512]{1,0:T(8,128)(2,1)S(1)} %collective-permute-done.next_ref), channel_id=1, source_target_pairs={{0,12},{4,8},{8,4},{12,0},{1,13},{5,9},{9,5},{13,1},{2,14},{6,10},... | collective-permute-start | bytes 294920 | tf_op jit(solution)/shard_map/ppermute | solution.py:289
  55.6 19.9 %copy-start = (f32[32,256]{1,0:T(8,128)S(1)}, f32[32,256]{1,0:T(8,128)}, u32[]{:S(2)}) copy-start(f32[32,256]{1,0:T(8,128)} %d_ref.5) | copy-start | bytes 98308
  55.6 19.9 %copy-start.1 = (f32[32,256]{1,0:T(8,128)S(1)}, f32[32,256]{1,0:T(8,128)}, u32[]{:S(2)}) copy-start(f32[32,256]{1,0:T(8,128)} %r_ref.3) | copy-start | bytes 98308
  55.6 41.3 %copy-start.2 = (f32[32,256]{1,0:T(8,128)S(1)}, f32[32,256]{1,0:T(8,128)}, u32[]{:S(2)}) copy-start(f32[32,256]{1,0:T(8,128)} %coeffs_ref.1) | copy-start | bytes 98308

commit v6 on v5

--- a/solution.py
+++ b/solution.py
@@ -227,9 +227,11 @@
 
 def gathered(parts_ref):
     low = high = 0.0
-    for i in range(N_SPLIT):
-        power = jnp.broadcast_to(parts_ref[i, 2 * TGT:2 * TGT + 1, :], (HALF, HALF)).T[:TGT]
-        back = jnp.exp2(power - 15.0)
+    powers = jnp.concatenate([parts_ref[i, 2 * TGT:2 * TGT + 1, :] for i in range(N_SPLIT)], axis=0)
+    backs = jnp.exp2(powers - 15.0)
+    backs = jnp.concatenate([backs, jnp.zeros((HALF - N_SPLIT, HALF), F32)], axis=0).T[:TGT]
+    for i in range(N_SPLIT):
+        back = jnp.broadcast_to(backs[:, i:i + 1], (TGT, HALF))
         low = low + parts_ref[i, :TGT, :] * back
         high = high + parts_ref[i, TGT:2 * TGT, :] * back
     return jnp.concatenate([low, high], axis=1)
@@ -293,7 +295,7 @@
     x = lax.axis_index("x").reshape(1)
     dirs, own, cens = first_copies(x, direction, episodes, centers)
     near = from_x(own, 1)
-    far = from_x(near, 3), from_x(near, 2)
+    far = from_x(near, 3), from_x(own, 3)
     dirs = exchange(dirs, SPLIT)
     early, right = early_tiles(own, near, cens)
     kmat, row_parts = tiles_and_rows(x, far, right, early, dirs)

time: 98.2 us -> 97.6 us (level)
  blocking collectives: 61 us -> 58.6 us
  waiting for transfers between devices: 2.86 us -> 4.63 us
    all_to_all x1, waiting for transfers between devices: 1.23 us -> 4.57 us  [exchange(): return here(lax.all_to_all(here(x), axes, 0, 0, tiled=False))]
    ppermute x3, waiting for transfers between devices: 1.62 us -> 0.07 us  [from_x(): return lax.ppermute(v, 'x', [(k, k ^ m) for k in range(N_X)])]
    all_to_all x2, blocking collectives: 23.5 us -> 22.1 us  [exchange(): return here(lax.all_to_all(here(x), axes, 0, 0, tiled=False))]
    all_to_all x1, blocking collectives: 16.7 us -> 15.6 us  [shards(): parts = lax.all_to_all(parts, SPLIT, 0, 0, tiled=False).astype(F32)]
where the time goes in v6:
time: 97.6 us; the launch traced here: 97.2 us
  blocking collectives  58.6 us (60%)
  Pallas kernels  17.3 us (18%)
  starting transfers between devices  15.8 us (16%)
  waiting for transfers between devices  4.63 us (5%)
    all_to_all x2, blocking collectives, exchange(): return here(lax.all_to_all(here(x), axes, 0, 0, tiled=False))  22.1 us
    all_to_all x1, blocking collectives, shards(): lax.all_to_all(sums.reshape(256, 1, 4 * TGT), AXES, 0, 0, tiled=False)  20.9 us
    all_to_all x1, blocking collectives, shards(): parts = lax.all_to_all(parts, SPLIT, 0, 0, tiled=False).astype(F32)  15.6 us
    all_to_all x1, starting transfers between devices, exchange(): return here(lax.all_to_all(here(x), axes, 0, 0, tiled=False))  10.9 us
    pallas_call x1, Pallas kernels, tiles_and_rows(): pl.pallas_call(late_kernel, in_specs=[IN_SMEM] + [IN_VMEM] * 3 + [ANYWHER...  7 us
    ppermute x3, starting transfers between devices, from_x(): return lax.ppermute(v, 'x', [(k, k ^ m) for k in range(N_X)])  4.89 us
    all_to_all x1, waiting for transfers between devices, exchange(): return here(lax.all_to_all(here(x), axes, 0, 0, tiled=False))  4.57 us
    pallas_call x1, Pallas kernels, early_tiles(): pl.pallas_call(early_kernel, in_specs=[IN_VMEM] * 3, out_specs=(ANYWHERE,...  3.74 us
  transfers between devices with their start and end apart: 4, of which 2 were waited for; matrix products, arithmetic and copies ran while one was open for 0% of the time, Pallas kernels for 4%

profile of v6, /device:TPU:1, one launch (start us, length us, event | category | flops | bytes accessed | tf_op | source)
XLA Modules:
  0.0 97.2 jit_solution(18433416209969376823)
XLA Ops:
  0.6 2.1 %shard_map.76 = (bf16[16,32,256]{2,1,0:T(8,128)(2,1)}, bf16[96,512]{1,0:T(8,128)(2,1)S(1)}, bf16[16,96,256]{2,1,0:T(8,128)(2,1)S(1)}) custom-call(s32[1]{0:T(128)} %bitcast.place_ref.x_ref, f32[32,256]{1,0:T(8,128)} %d_ref.5, bf16[96,512]{1,0:T(8,128)(2,1)} %e_ref.1, bf16[96,16384]{1,0:T(8,128)(2,1)} %cen_ref.1), custom_call_target="tpu_custom_call" | custom-call | tf_op jit(solution)/shard_map/pallas_call | solution.py:82
  2.7 2.1 %collective-permute-start = (bf16[96,512]{1,0:T(8,128)(2,1)S(1)}, bf16[96,512]{1,0:T(8,128)(2,1)S(1)}, u32[]{:S(2)}, u32[]{:S(2)}) collective-permute-start(bf16[96,512]{1,0:T(8,128)(2,1)S(1)} %get-tuple-element.12.own_ref), channel_id=1, source_target_pairs={{0,4},{4,0},{8,12},{12,8},{1,5},{5,1},{9,13},{13,9},{2,6},{6,2},{1... | collective-permute-start | bytes 294920 | tf_op jit(solution)/shard_map/ppermute | solution.py:291
  4.8 1.8 %collective-permute-start.2 = (bf16[96,512]{1,0:T(8,128)(2,1)S(1)}, bf16[96,512]{1,0:T(8,128)(2,1)S(1)}, u32[]{:S(2)}, u32[]{:S(2)}) collective-permute-start(bf16[96,512]{1,0:T(8,128)(2,1)S(1)} %get-tuple-element.12.own_ref), channel_id=1, source_target_pairs={{0,12},{4,8},{8,4},{12,0},{1,13},{5,9},{9,5},{13,1},{2,14},{6,10},... | collective-permute-start | bytes 294920 | tf_op jit(solution)/shard_map/ppermute | solution.py:291
  6.6 10.9 %all-to-all-start = ((bf16[16,32,256]{2,1,0:T(8,128)(2,1)}), bf16[16,32,256]{2,1,0:T(8,128)(2,1)S(1)}, u32[]{:S(2)}, u32[]{:S(2)}) async-start(bf16[16,32,256]{2,1,0:T(8,128)(2,1)} %get-tuple-element.16), calls=%async_computation | async-start | bytes 524288 | tf_op jit(solution)/shard_map/all_to_all | solution.py:49
  17.6 0.0 collective-permute-done.next_ref
  17.6 0.9 collective-permute-start.1
  18.5 3.7 %shard_map.77 = (bf16[16,1024,256]{2,1,0:T(8,128)(2,1)}, bf16[16,128,256]{2,1,0:T(8,128)(2,1)S(1)}) custom-call(bf16[96,512]{1,0:T(8,128)(2,1)S(1)} %get-tuple-element.12.own_ref, bf16[96,512]{1,0:T(8,128)(2,1)S(1)} %collective-permute-done.next_ref, bf16[16,96,256]{2,1,0:T(8,128)(2,1)S(1)} %get-tuple-element.13.cens), custom_call_target="tpu_custom_call" | custom-call | flops 99999997952 | bytes 8388608 | tf_op jit(solution)/shard_map/pallas_call | solution.py:126
  22.3 0.0 collective-permute-done.2.p3_ref
  22.3 0.1 collective-permute-done.1.p2_ref
  22.3 4.6 %all-to-all-done.d_ref = bf16[16,32,256]{2,1,0:T(8,128)(2,1)S(1)} async-done(((bf16[16,32,256]{2,1,0:T(8,128)(2,1)}), bf16[16,32,256]{2,1,0:T(8,128)(2,1)S(1)}, u32[]{:S(2)}, u32[]{:S(2)}) %all-to-all-start) | async-done | bytes 262176 | tf_op jit(solution)/shard_map/all_to_all | solution.py:49
  26.9 7.0 %shard_map.78 = (bf16[16,2048,256]{2,1,0:T(8,128)(2,1)S(1)}, f32[16,32,128]{2,1,0:T(8,128)S(1)}) custom-call(s32[1]{0:T(128)} %bitcast.place_ref.x_ref, bf16[96,512]{1,0:T(8,128)(2,1)S(1)} %collective-permute-done.1.p2_ref, bf16[96,512]{1,0:T(8,128)(2,1)S(1)} %collective-permute-done.2.p3_ref, bf16[16,128,256]{2,1,0:T(8,128)(2,1)S(1)} %get-tuple-element.14.right_ref, ...), custom_call_target="tpu_custom_call" | custom-call | flops 2684354560 | bytes 16777216 | tf_op jit(solution)/shard_map/pallas_call | solution.py:167
  33.9 13.1 %all_to_all.25.parts_ref = f32[16,32,128]{2,1,0:T(8,128)S(1)} all-to-all(f32[16,32,128]{2,1,0:T(8,128)S(1)} %get-tuple-element.17), channel_id=1, replica_groups=mesh['yh'=2,'z'=8,'x'=4,'yl'=2,'c'=2] {'x','yl','c'}, dimensions={0} | all-to-all | bytes 524288 | tf_op jit(solution)/shard_map/all_to_all | solution.py:49
  47.0 9.1 %all_to_all.26.rows_ref = bf16[16,32,128]{2,1,0:T(8,128)(2,1)S(1)} all-to-all(bf16[16,32,128]{2,1,0:T(8,128)(2,1)S(1)} %shard_map.79), channel_id=1, replica_groups=mesh['yh'=2,'z'=8,'x'=4,'yl'=2,'c'=2] {'x','yl','c'}, dimensions={0} | all-to-all | bytes 262144 | tf_op jit(solution)/shard_map/all_to_all | solution.py:49
  56.1 0.0 copy-start
  56.1 0.0 copy-start.1
  56.1 0.0 copy-start.2
  56.1 3.1 %shard_map.80 = f32[16,72,128]{2,1,0:T(8,128)S(1)} custom-call(s32[1]{0:T(128)} %bitcast.place_ref.x_ref, bf16[16,32,128]{2,1,0:T(8,128)(2,1)S(1)} %all_to_all.26.rows_ref, bf16[16,2048,256]{2,1,0:T(8,128)(2,1)S(1)} %get-tuple-element.18.k_ref), custom_call_target="tpu_custom_call" | custom-call | flops 536870912 | bytes 16777216 | tf_op jit(solution)/shard_map/pallas_call | solution.py:217
  59.3 15.6 %all_to_all.27 = f16[16,72,128]{2,1,0:T(8,128)(2,1)S(1)} all-to-all(f16[16,72,128]{2,1,0:T(8,128)(2,1)S(1)} %convert_element_type.6), channel_id=1, replica_groups=mesh['yh'=2,'z'=8,'x'=4,'yl'=2,'c'=2] {'yh','z'}, dimensions={0} | all-to-all | bytes 589824 | tf_op jit(solution)/shard_map/all_to_all | solution.py:305
  74.9 0.0 copy-done
  74.9 0.0 copy-done.1
  74.9 0.5 shard_map.81
  75.4 20.9 %all_to_all.28 = f32[256,1,128]{2,1,0:T(1,128)S(1)} all-to-all(f32[256,1,128]{2,1,0:T(1,128)S(1)} %bitcast.6), channel_id=1, replica_groups=mesh['yh'=2,'z'=8,'x'=4,'yl'=2,'c'=2] {'yh','z','x','yl','c'}, dimensions={0} | all-to-all | bytes 262144 | tf_op jit(solution)/shard_map/all_to_all | solution.py:307
  96.3 0.0 copy-done.2
  96.3 0.9 shard_map.82
  (3 shorter events, 0.1 us)
Async XLA Ops:
  2.7 14.9 %collective-permute-start = (bf16[96,512]{1,0:T(8,128)(2,1)S(1)}, bf16[96,512]{1,0:T(8,128)(2,1)S(1)}, u32[]{:S(2)}, u32[]{:S(2)}) collective-permute-start(bf16[96,512]{1,0:T(8,128)(2,1)S(1)} %get-tuple-element.12.own_ref), channel_id=1, source_target_pairs={{0,4},{4,0},{8,12},{12,8},{1,5},{5,1},{9,13},{13,9},{2,6},{6,2},{1... | collective-permute-start | bytes 294920 | tf_op jit(solution)/shard_map/ppermute | solution.py:291
  4.8 17.5 %collective-permute-start.2 = (bf16[96,512]{1,0:T(8,128)(2,1)S(1)}, bf16[96,512]{1,0:T(8,128)(2,1)S(1)}, u32[]{:S(2)}, u32[]{:S(2)}) collective-permute-start(bf16[96,512]{1,0:T(8,128)(2,1)S(1)} %get-tuple-element.12.own_ref), channel_id=1, source_target_pairs={{0,12},{4,8},{8,4},{12,0},{1,13},{5,9},{9,5},{13,1},{2,14},{6,10},... | collective-permute-start | bytes 294920 | tf_op jit(solution)/shard_map/ppermute | solution.py:291
  6.6 20.3 %all-to-all-start = ((bf16[16,32,256]{2,1,0:T(8,128)(2,1)}), bf16[16,32,256]{2,1,0:T(8,128)(2,1)S(1)}, u32[]{:S(2)}, u32[]{:S(2)}) async-start(bf16[16,32,256]{2,1,0:T(8,128)(2,1)} %get-tuple-element.16), calls=%async_computation | async-start | bytes 524288 | tf_op jit(solution)/shard_map/all_to_all | solution.py:49
  17.6 4.8 %collective-permute-start.1 = (bf16[96,512]{1,0:T(8,128)(2,1)S(1)}, bf16[96,512]{1,0:T(8,128)(2,1)S(1)}, u32[]{:S(2)}, u32[]{:S(2)}) collective-permute-start(bf16[96,512]{1,0:T(8,128)(2,1)S(1)} %collective-permute-done.next_ref), channel_id=1, source_target_pairs={{0,12},{4,8},{8,4},{12,0},{1,13},{5,9},{9,5},{13,1},{2,14},{6,10},... | collective-permute-start | bytes 294920 | tf_op jit(solution)/shard_map/ppermute | solution.py:291
  56.1 18.8 %copy-start = (f32[32,256]{1,0:T(8,128)S(1)}, f32[32,256]{1,0:T(8,128)}, u32[]{:S(2)}) copy-start(f32[32,256]{1,0:T(8,128)} %d_ref.5) | copy-start | bytes 98308
  56.1 18.8 %copy-start.1 = (f32[32,256]{1,0:T(8,128)S(1)}, f32[32,256]{1,0:T(8,128)}, u32[]{:S(2)}) copy-start(f32[32,256]{1,0:T(8,128)} %r_ref.3) | copy-start | bytes 98308
  56.1 40.2 %copy-start.2 = (f32[32,256]{1,0:T(8,128)S(1)}, f32[32,256]{1,0:T(8,128)}, u32[]{:S(2)}) copy-start(f32[32,256]{1,0:T(8,128)} %coeffs_ref.1) | copy-start | bytes 98308

commit v7 on v6

--- a/solution.py
+++ b/solution.py
@@ -295,7 +295,8 @@
     x = lax.axis_index("x").reshape(1)
     dirs, own, cens = first_copies(x, direction, episodes, centers)
     near = from_x(own, 1)
-    far = from_x(near, 3), from_x(own, 3)
+    late_own, late_near = lax.optimization_barrier((own, near))
+    far = from_x(late_near, 3), from_x(late_own, 3)
     dirs = exchange(dirs, SPLIT)
     early, right = early_tiles(own, near, cens)
     kmat, row_parts = tiles_and_rows(x, far, right, early, dirs)
@@ -304,7 +305,7 @@
     parts = column_sums(x, rows, kmat).astype(F16)
     parts = lax.all_to_all(parts, SPLIT, 0, 0, tiled=False).astype(F32)
     applied, sums = apply_and_sum(parts, residual, direction)
-    sums = lax.all_to_all(sums.reshape(256, 1, 4 * TGT), AXES, 0, 0, tiled=False).reshape(256, 4 * TGT)
+    sums = lax.all_to_all(sums.reshape(256, 1, 4 * TGT), AXES[::-1], 0, 0, tiled=False).reshape(256, 4 * TGT)
     return step_and_update(sums, coeffs, residual, direction, applied)
 
 

time: 97.6 us -> 97.2 us (level)
  waiting for transfers between devices: 4.63 us -> 2.82 us
  blocking collectives: 58.6 us -> 60 us
    all_to_all x1, waiting for transfers between devices: 4.57 us -> 1.53 us  [exchange(): return here(lax.all_to_all(here(x), axes, 0, 0, tiled=False))]
    all_to_all x2, blocking collectives: 22.1 us -> 23.5 us  [exchange(): return here(lax.all_to_all(here(x), axes, 0, 0, tiled=False))]
    ppermute x3, waiting for transfers between devices: 0.07 us -> 1.29 us  [from_x(): return lax.ppermute(v, 'x', [(k, k ^ m) for k in range(N_X)])]
where the time goes in v7:
time: 97.2 us; the launch traced here: 96.8 us
  blocking collectives  60 us (62%)
  Pallas kernels  17.4 us (18%)
  starting transfers between devices  15.8 us (16%)
  waiting for transfers between devices  2.82 us (3%)
    all_to_all x2, blocking collectives, exchange(): return here(lax.all_to_all(here(x), axes, 0, 0, tiled=False))  23.5 us
    all_to_all x1, blocking collectives, shards(): lax.all_to_all(sums.reshape(256, 1, 4 * TGT), AXES[::-1], 0, 0, tiled=False)  20.5 us
    all_to_all x1, blocking collectives, shards(): parts = lax.all_to_all(parts, SPLIT, 0, 0, tiled=False).astype(F32)  16.1 us
    all_to_all x1, starting transfers between devices, exchange(): return here(lax.all_to_all(here(x), axes, 0, 0, tiled=False))  10.9 us
    pallas_call x1, Pallas kernels, tiles_and_rows(): pl.pallas_call(late_kernel, in_specs=[IN_SMEM] + [IN_VMEM] * 3 + [ANYWHER...  7.01 us
    ppermute x3, starting transfers between devices, from_x(): return lax.ppermute(v, 'x', [(k, k ^ m) for k in range(N_X)])  4.89 us
    pallas_call x1, Pallas kernels, early_tiles(): pl.pallas_call(early_kernel, in_specs=[IN_VMEM] * 3, out_specs=(ANYWHERE,...  3.74 us
    pallas_call x1, Pallas kernels, column_sums(): pl.pallas_call(column_kernel, in_specs=[IN_SMEM] + [IN_VMEM] * 2, out_spe...  3.12 us
  transfers between devices with their start and end apart: 4, of which 2 were waited for; matrix products, arithmetic and copies ran while one was open for 0% of the time, Pallas kernels for 4%

profile of v7, /device:TPU:1, one launch (start us, length us, event | category | flops | bytes accessed | tf_op | source)
XLA Modules:
  0.0 96.8 jit_solution(5554375778150274776)
XLA Ops:
  0.6 2.1 %shard_map.76 = (bf16[16,32,256]{2,1,0:T(8,128)(2,1)}, bf16[96,512]{1,0:T(8,128)(2,1)S(1)}, bf16[16,96,256]{2,1,0:T(8,128)(2,1)S(1)}) custom-call(s32[1]{0:T(128)} %bitcast.place_ref.x_ref, f32[32,256]{1,0:T(8,128)} %d_ref.5, bf16[96,512]{1,0:T(8,128)(2,1)} %e_ref.1, bf16[96,16384]{1,0:T(8,128)(2,1)} %cen_ref.1), custom_call_target="tpu_custom_call" | custom-call | tf_op jit(solution)/shard_map/pallas_call | solution.py:82
  2.7 2.1 %collective-permute-start = (bf16[96,512]{1,0:T(8,128)(2,1)S(1)}, bf16[96,512]{1,0:T(8,128)(2,1)S(1)}, u32[]{:S(2)}, u32[]{:S(2)}) collective-permute-start(bf16[96,512]{1,0:T(8,128)(2,1)S(1)} %get-tuple-element.16.own_ref), channel_id=1, source_target_pairs={{0,4},{4,0},{8,12},{12,8},{1,5},{5,1},{9,13},{13,9},{2,6},{6,2},{1... | collective-permute-start | bytes 294920 | tf_op jit(solution)/shard_map/ppermute | solution.py:291
  4.8 10.9 %all-to-all-start = ((bf16[16,32,256]{2,1,0:T(8,128)(2,1)}), bf16[16,32,256]{2,1,0:T(8,128)(2,1)S(1)}, u32[]{:S(2)}, u32[]{:S(2)}) async-start(bf16[16,32,256]{2,1,0:T(8,128)(2,1)} %get-tuple-element.20), calls=%async_computation | async-start | bytes 524288 | tf_op jit(solution)/shard_map/all_to_all | solution.py:49
  15.8 0.0 collective-permute-done.next_ref
  15.8 1.9 %collective-permute-start.1 = (bf16[96,512]{1,0:T(8,128)(2,1)S(1)}, bf16[96,512]{1,0:T(8,128)(2,1)S(1)}, u32[]{:S(2)}, u32[]{:S(2)}) collective-permute-start(bf16[96,512]{1,0:T(8,128)(2,1)S(1)} %collective-permute-done.next_ref), channel_id=1, source_target_pairs={{0,12},{4,8},{8,4},{12,0},{1,13},{5,9},{9,5},{13,1},{2,14},{6,10},... | collective-permute-start | bytes 294920 | tf_op jit(solution)/shard_map/ppermute | solution.py:291
  17.7 0.9 collective-permute-start.2
  18.5 3.7 %shard_map.77 = (bf16[16,1024,256]{2,1,0:T(8,128)(2,1)}, bf16[16,128,256]{2,1,0:T(8,128)(2,1)S(1)}) custom-call(bf16[96,512]{1,0:T(8,128)(2,1)S(1)} %get-tuple-element.16.own_ref, bf16[96,512]{1,0:T(8,128)(2,1)S(1)} %collective-permute-done.next_ref, bf16[16,96,256]{2,1,0:T(8,128)(2,1)S(1)} %get-tuple-element.17.cens), custom_call_target="tpu_custom_call" | custom-call | flops 99999997952 | bytes 8388608 | tf_op jit(solution)/shard_map/pallas_call | solution.py:126
  22.3 0.0 collective-permute-done.1.p2_ref
  22.3 1.3 %collective-permute-done.2.p3_ref = bf16[96,512]{1,0:T(8,128)(2,1)S(1)} collective-permute-done((bf16[96,512]{1,0:T(8,128)(2,1)S(1)}, bf16[96,512]{1,0:T(8,128)(2,1)S(1)}, u32[]{:S(2)}, u32[]{:S(2)}) %collective-permute-start.2) | collective-permute-done | bytes 98336 | tf_op jit(solution)/shard_map/ppermute | solution.py:291
  23.6 1.5 %all-to-all-done.d_ref = bf16[16,32,256]{2,1,0:T(8,128)(2,1)S(1)} async-done(((bf16[16,32,256]{2,1,0:T(8,128)(2,1)}), bf16[16,32,256]{2,1,0:T(8,128)(2,1)S(1)}, u32[]{:S(2)}, u32[]{:S(2)}) %all-to-all-start) | async-done | bytes 262176 | tf_op jit(solution)/shard_map/all_to_all | solution.py:49
  25.1 7.0 %shard_map.78 = (bf16[16,2048,256]{2,1,0:T(8,128)(2,1)S(1)}, f32[16,32,128]{2,1,0:T(8,128)S(1)}) custom-call(s32[1]{0:T(128)} %bitcast.place_ref.x_ref, bf16[96,512]{1,0:T(8,128)(2,1)S(1)} %collective-permute-done.1.p2_ref, bf16[96,512]{1,0:T(8,128)(2,1)S(1)} %collective-permute-done.2.p3_ref, bf16[16,128,256]{2,1,0:T(8,128)(2,1)S(1)} %get-tuple-element.18.right_ref, ...), custom_call_target="tpu_custom_call" | custom-call | flops 2684354560 | bytes 16777216 | tf_op jit(solution)/shard_map/pallas_call | solution.py:167
  32.1 14.4 %all_to_all.25.parts_ref = f32[16,32,128]{2,1,0:T(8,128)S(1)} all-to-all(f32[16,32,128]{2,1,0:T(8,128)S(1)} %get-tuple-element.21), channel_id=1, replica_groups=mesh['yh'=2,'z'=8,'x'=4,'yl'=2,'c'=2] {'x','yl','c'}, dimensions={0} | all-to-all | bytes 524288 | tf_op jit(solution)/shard_map/all_to_all | solution.py:49
  46.6 9.0 %all_to_all.26.rows_ref = bf16[16,32,128]{2,1,0:T(8,128)(2,1)S(1)} all-to-all(bf16[16,32,128]{2,1,0:T(8,128)(2,1)S(1)} %shard_map.79), channel_id=1, replica_groups=mesh['yh'=2,'z'=8,'x'=4,'yl'=2,'c'=2] {'x','yl','c'}, dimensions={0} | all-to-all | bytes 262144 | tf_op jit(solution)/shard_map/all_to_all | solution.py:49
  55.6 0.0 copy-start
  55.6 0.0 copy-start.1
  55.6 0.0 copy-start.2
  55.6 3.1 %shard_map.80 = f32[16,72,128]{2,1,0:T(8,128)S(1)} custom-call(s32[1]{0:T(128)} %bitcast.place_ref.x_ref, bf16[16,32,128]{2,1,0:T(8,128)(2,1)S(1)} %all_to_all.26.rows_ref, bf16[16,2048,256]{2,1,0:T(8,128)(2,1)S(1)} %get-tuple-element.22.k_ref), custom_call_target="tpu_custom_call" | custom-call | flops 536870912 | bytes 16777216 | tf_op jit(solution)/shard_map/pallas_call | solution.py:217
  58.8 16.1 %all_to_all.27 = f16[16,72,128]{2,1,0:T(8,128)(2,1)S(1)} all-to-all(f16[16,72,128]{2,1,0:T(8,128)(2,1)S(1)} %convert_element_type.6), channel_id=1, replica_groups=mesh['yh'=2,'z'=8,'x'=4,'yl'=2,'c'=2] {'yh','z'}, dimensions={0} | all-to-all | bytes 589824 | tf_op jit(solution)/shard_map/all_to_all | solution.py:306
  74.9 0.0 copy-done
  74.9 0.0 copy-done.1
  74.9 0.5 shard_map.81
  75.4 20.5 %all_to_all.28 = f32[256,1,128]{2,1,0:T(1,128)S(1)} all-to-all(f32[256,1,128]{2,1,0:T(1,128)S(1)} %bitcast.6), channel_id=1, replica_groups=mesh['yh'=2,'z'=8,'x'=4,'yl'=2,'c'=2] {'c','yl','x','z','yh'}, dimensions={0} | all-to-all | bytes 262144 | tf_op jit(solution)/shard_map/all_to_all | solution.py:308
  95.9 0.0 copy-done.2
  95.9 0.9 shard_map.82
  (3 shorter events, 0.1 us)
Async XLA Ops:
  2.7 13.1 %collective-permute-start = (bf16[96,512]{1,0:T(8,128)(2,1)S(1)}, bf16[96,512]{1,0:T(8,128)(2,1)S(1)}, u32[]{:S(2)}, u32[]{:S(2)}) collective-permute-start(bf16[96,512]{1,0:T(8,128)(2,1)S(1)} %get-tuple-element.16.own_ref), channel_id=1, source_target_pairs={{0,4},{4,0},{8,12},{12,8},{1,5},{5,1},{9,13},{13,9},{2,6},{6,2},{1... | collective-permute-start | bytes 294920 | tf_op jit(solution)/shard_map/ppermute | solution.py:291
  4.8 20.3 %all-to-all-start = ((bf16[16,32,256]{2,1,0:T(8,128)(2,1)}), bf16[16,32,256]{2,1,0:T(8,128)(2,1)S(1)}, u32[]{:S(2)}, u32[]{:S(2)}) async-start(bf16[16,32,256]{2,1,0:T(8,128)(2,1)} %get-tuple-element.20), calls=%async_computation | async-start | bytes 524288 | tf_op jit(solution)/shard_map/all_to_all | solution.py:49
  15.8 6.5 %collective-permute-start.1 = (bf16[96,512]{1,0:T(8,128)(2,1)S(1)}, bf16[96,512]{1,0:T(8,128)(2,1)S(1)}, u32[]{:S(2)}, u32[]{:S(2)}) collective-permute-start(bf16[96,512]{1,0:T(8,128)(2,1)S(1)} %collective-permute-done.next_ref), channel_id=1, source_target_pairs={{0,12},{4,8},{8,4},{12,0},{1,13},{5,9},{9,5},{13,1},{2,14},{6,10},... | collective-permute-start | bytes 294920 | tf_op jit(solution)/shard_map/ppermute | solution.py:291
  17.7 5.9 %collective-permute-start.2 = (bf16[96,512]{1,0:T(8,128)(2,1)S(1)}, bf16[96,512]{1,0:T(8,128)(2,1)S(1)}, u32[]{:S(2)}, u32[]{:S(2)}) collective-permute-start(bf16[96,512]{1,0:T(8,128)(2,1)S(1)} %get-tuple-element.16.own_ref), channel_id=1, source_target_pairs={{0,12},{4,8},{8,4},{12,0},{1,13},{5,9},{9,5},{13,1},{2,14},{6,10},... | collective-permute-start | bytes 294920 | tf_op jit(solution)/shard_map/ppermute | solution.py:291
  55.6 19.3 %copy-start = (f32[32,256]{1,0:T(8,128)S(1)}, f32[32,256]{1,0:T(8,128)}, u32[]{:S(2)}) copy-start(f32[32,256]{1,0:T(8,128)} %d_ref.5) | copy-start | bytes 98308
  55.6 19.3 %copy-start.1 = (f32[32,256]{1,0:T(8,128)S(1)}, f32[32,256]{1,0:T(8,128)}, u32[]{:S(2)}) copy-start(f32[32,256]{1,0:T(8,128)} %r_ref.3) | copy-start | bytes 98308
  55.6 40.3 %copy-start.2 = (f32[32,256]{1,0:T(8,128)S(1)}, f32[32,256]{1,0:T(8,128)}, u32[]{:S(2)}) copy-start(f32[32,256]{1,0:T(8,128)} %coeffs_ref.1) | copy-start | bytes 98308

commit v8 on v7

--- a/solution.py
+++ b/solution.py
@@ -97,7 +97,7 @@
     e = e.astype(F32)
     norm = jnp.sum(e * e, axis=0, keepdims=True)
     tall = jnp.concatenate([e * (2.0 * SHARP), extra_rows(three(-SHARP * norm), 0, OWN)], axis=0)
-    return tall.T.astype(BF16)
+    return tall.astype(BF16).T
 
 
 def tile(left, right):

time: 97.2 us -> 97.2 us (level)
  no operation moved by 1% of the time
where the time goes in v8:
time: 97.2 us; the launch traced here: 96.9 us
  blocking collectives  60 us (62%)
  Pallas kernels  17.4 us (18%)
  starting transfers between devices  15.8 us (16%)
  waiting for transfers between devices  2.83 us (3%)
    all_to_all x2, blocking collectives, exchange(): return here(lax.all_to_all(here(x), axes, 0, 0, tiled=False))  23.5 us
    all_to_all x1, blocking collectives, shards(): lax.all_to_all(sums.reshape(256, 1, 4 * TGT), AXES[::-1], 0, 0, tiled=False)  20.5 us
    all_to_all x1, blocking collectives, shards(): parts = lax.all_to_all(parts, SPLIT, 0, 0, tiled=False).astype(F32)  16 us
    all_to_all x1, starting transfers between devices, exchange(): return here(lax.all_to_all(here(x), axes, 0, 0, tiled=False))  10.9 us
    pallas_call x1, Pallas kernels, tiles_and_rows(): pl.pallas_call(late_kernel, in_specs=[IN_SMEM] + [IN_VMEM] * 3 + [ANYWHER...  7.02 us
    ppermute x3, starting transfers between devices, from_x(): return lax.ppermute(v, 'x', [(k, k ^ m) for k in range(N_X)])  4.89 us
    pallas_call x1, Pallas kernels, early_tiles(): pl.pallas_call(early_kernel, in_specs=[IN_VMEM] * 3, out_specs=(ANYWHERE,...  3.73 us
    pallas_call x1, Pallas kernels, column_sums(): pl.pallas_call(column_kernel, in_specs=[IN_SMEM] + [IN_VMEM] * 2, out_spe...  3.12 us
  transfers between devices with their start and end apart: 4, of which 2 were waited for; matrix products, arithmetic and copies ran while one was open for 0% of the time, Pallas kernels for 4%

profile of v8, /device:TPU:1, one launch (start us, length us, event | category | flops | bytes accessed | tf_op | source)
XLA Modules:
  0.0 96.9 jit_solution(8018895859243679555)
XLA Ops:
  0.6 2.1 %shard_map.76 = (bf16[16,32,256]{2,1,0:T(8,128)(2,1)}, bf16[96,512]{1,0:T(8,128)(2,1)S(1)}, bf16[16,96,256]{2,1,0:T(8,128)(2,1)S(1)}) custom-call(s32[1]{0:T(128)} %bitcast.place_ref.x_ref, f32[32,256]{1,0:T(8,128)} %d_ref.5, bf16[96,512]{1,0:T(8,128)(2,1)} %e_ref.1, bf16[96,16384]{1,0:T(8,128)(2,1)} %cen_ref.1), custom_call_target="tpu_custom_call" | custom-call | tf_op jit(solution)/shard_map/pallas_call | solution.py:82
  2.7 2.1 %collective-permute-start = (bf16[96,512]{1,0:T(8,128)(2,1)S(1)}, bf16[96,512]{1,0:T(8,128)(2,1)S(1)}, u32[]{:S(2)}, u32[]{:S(2)}) collective-permute-start(bf16[96,512]{1,0:T(8,128)(2,1)S(1)} %get-tuple-element.16.own_ref), channel_id=1, source_target_pairs={{0,4},{4,0},{8,12},{12,8},{1,5},{5,1},{9,13},{13,9},{2,6},{6,2},{1... | collective-permute-start | bytes 294920 | tf_op jit(solution)/shard_map/ppermute | solution.py:291
  4.8 10.9 %all-to-all-start = ((bf16[16,32,256]{2,1,0:T(8,128)(2,1)}), bf16[16,32,256]{2,1,0:T(8,128)(2,1)S(1)}, u32[]{:S(2)}, u32[]{:S(2)}) async-start(bf16[16,32,256]{2,1,0:T(8,128)(2,1)} %get-tuple-element.20), calls=%async_computation | async-start | bytes 524288 | tf_op jit(solution)/shard_map/all_to_all | solution.py:49
  15.8 0.0 collective-permute-done.next_ref
  15.8 1.9 %collective-permute-start.1 = (bf16[96,512]{1,0:T(8,128)(2,1)S(1)}, bf16[96,512]{1,0:T(8,128)(2,1)S(1)}, u32[]{:S(2)}, u32[]{:S(2)}) collective-permute-start(bf16[96,512]{1,0:T(8,128)(2,1)S(1)} %collective-permute-done.next_ref), channel_id=1, source_target_pairs={{0,12},{4,8},{8,4},{12,0},{1,13},{5,9},{9,5},{13,1},{2,14},{6,10},... | collective-permute-start | bytes 294920 | tf_op jit(solution)/shard_map/ppermute | solution.py:291
  17.7 0.9 collective-permute-start.2
  18.5 3.7 %shard_map.77 = (bf16[16,1024,256]{2,1,0:T(8,128)(2,1)}, bf16[16,128,256]{2,1,0:T(8,128)(2,1)S(1)}) custom-call(bf16[96,512]{1,0:T(8,128)(2,1)S(1)} %get-tuple-element.16.own_ref, bf16[96,512]{1,0:T(8,128)(2,1)S(1)} %collective-permute-done.next_ref, bf16[16,96,256]{2,1,0:T(8,128)(2,1)S(1)} %get-tuple-element.17.cens), custom_call_target="tpu_custom_call" | custom-call | flops 99999997952 | bytes 8388608 | tf_op jit(solution)/shard_map/pallas_call | solution.py:126
  22.3 0.0 collective-permute-done.1.p2_ref
  22.3 1.3 %collective-permute-done.2.p3_ref = bf16[96,512]{1,0:T(8,128)(2,1)S(1)} collective-permute-done((bf16[96,512]{1,0:T(8,128)(2,1)S(1)}, bf16[96,512]{1,0:T(8,128)(2,1)S(1)}, u32[]{:S(2)}, u32[]{:S(2)}) %collective-permute-start.2) | collective-permute-done | bytes 98336 | tf_op jit(solution)/shard_map/ppermute | solution.py:291
  23.6 1.5 %all-to-all-done.d_ref = bf16[16,32,256]{2,1,0:T(8,128)(2,1)S(1)} async-done(((bf16[16,32,256]{2,1,0:T(8,128)(2,1)}), bf16[16,32,256]{2,1,0:T(8,128)(2,1)S(1)}, u32[]{:S(2)}, u32[]{:S(2)}) %all-to-all-start) | async-done | bytes 262176 | tf_op jit(solution)/shard_map/all_to_all | solution.py:49
  25.1 7.0 %shard_map.78 = (bf16[16,2048,256]{2,1,0:T(8,128)(2,1)S(1)}, f32[16,32,128]{2,1,0:T(8,128)S(1)}) custom-call(s32[1]{0:T(128)} %bitcast.place_ref.x_ref, bf16[96,512]{1,0:T(8,128)(2,1)S(1)} %collective-permute-done.1.p2_ref, bf16[96,512]{1,0:T(8,128)(2,1)S(1)} %collective-permute-done.2.p3_ref, bf16[16,128,256]{2,1,0:T(8,128)(2,1)S(1)} %get-tuple-element.18.right_ref, ...), custom_call_target="tpu_custom_call" | custom-call | flops 2684354560 | bytes 16777216 | tf_op jit(solution)/shard_map/pallas_call | solution.py:167
  32.1 14.4 %all_to_all.25.parts_ref = f32[16,32,128]{2,1,0:T(8,128)S(1)} all-to-all(f32[16,32,128]{2,1,0:T(8,128)S(1)} %get-tuple-element.21), channel_id=1, replica_groups=mesh['yh'=2,'z'=8,'x'=4,'yl'=2,'c'=2] {'x','yl','c'}, dimensions={0} | all-to-all | bytes 524288 | tf_op jit(solution)/shard_map/all_to_all | solution.py:49
  46.6 9.0 %all_to_all.26.rows_ref = bf16[16,32,128]{2,1,0:T(8,128)(2,1)S(1)} all-to-all(bf16[16,32,128]{2,1,0:T(8,128)(2,1)S(1)} %shard_map.79), channel_id=1, replica_groups=mesh['yh'=2,'z'=8,'x'=4,'yl'=2,'c'=2] {'x','yl','c'}, dimensions={0} | all-to-all | bytes 262144 | tf_op jit(solution)/shard_map/all_to_all | solution.py:49
  55.7 0.0 copy-start
  55.7 0.0 copy-start.1
  55.7 0.0 copy-start.2
  55.7 3.1 %shard_map.80 = f32[16,72,128]{2,1,0:T(8,128)S(1)} custom-call(s32[1]{0:T(128)} %bitcast.place_ref.x_ref, bf16[16,32,128]{2,1,0:T(8,128)(2,1)S(1)} %all_to_all.26.rows_ref, bf16[16,2048,256]{2,1,0:T(8,128)(2,1)S(1)} %get-tuple-element.22.k_ref), custom_call_target="tpu_custom_call" | custom-call | flops 536870912 | bytes 16777216 | tf_op jit(solution)/shard_map/pallas_call | solution.py:217
  58.8 16.0 %all_to_all.27 = f16[16,72,128]{2,1,0:T(8,128)(2,1)S(1)} all-to-all(f16[16,72,128]{2,1,0:T(8,128)(2,1)S(1)} %convert_element_type.6), channel_id=1, replica_groups=mesh['yh'=2,'z'=8,'x'=4,'yl'=2,'c'=2] {'yh','z'}, dimensions={0} | all-to-all | bytes 589824 | tf_op jit(solution)/shard_map/all_to_all | solution.py:306
  74.9 0.0 copy-done
  74.9 0.0 copy-done.1
  74.9 0.5 shard_map.81
  75.4 20.5 %all_to_all.28 = f32[256,1,128]{2,1,0:T(1,128)S(1)} all-to-all(f32[256,1,128]{2,1,0:T(1,128)S(1)} %bitcast.6), channel_id=1, replica_groups=mesh['yh'=2,'z'=8,'x'=4,'yl'=2,'c'=2] {'c','yl','x','z','yh'}, dimensions={0} | all-to-all | bytes 262144 | tf_op jit(solution)/shard_map/all_to_all | solution.py:308
  95.9 0.0 copy-done.2
  95.9 0.9 shard_map.82
  (3 shorter events, 0.1 us)
Async XLA Ops:
  2.7 13.1 %collective-permute-start = (bf16[96,512]{1,0:T(8,128)(2,1)S(1)}, bf16[96,512]{1,0:T(8,128)(2,1)S(1)}, u32[]{:S(2)}, u32[]{:S(2)}) collective-permute-start(bf16[96,512]{1,0:T(8,128)(2,1)S(1)} %get-tuple-element.16.own_ref), channel_id=1, source_target_pairs={{0,4},{4,0},{8,12},{12,8},{1,5},{5,1},{9,13},{13,9},{2,6},{6,2},{1... | collective-permute-start | bytes 294920 | tf_op jit(solution)/shard_map/ppermute | solution.py:291
  4.8 20.3 %all-to-all-start = ((bf16[16,32,256]{2,1,0:T(8,128)(2,1)}), bf16[16,32,256]{2,1,0:T(8,128)(2,1)S(1)}, u32[]{:S(2)}, u32[]{:S(2)}) async-start(bf16[16,32,256]{2,1,0:T(8,128)(2,1)} %get-tuple-element.20), calls=%async_computation | async-start | bytes 524288 | tf_op jit(solution)/shard_map/all_to_all | solution.py:49
  15.8 6.5 %collective-permute-start.1 = (bf16[96,512]{1,0:T(8,128)(2,1)S(1)}, bf16[96,512]{1,0:T(8,128)(2,1)S(1)}, u32[]{:S(2)}, u32[]{:S(2)}) collective-permute-start(bf16[96,512]{1,0:T(8,128)(2,1)S(1)} %collective-permute-done.next_ref), channel_id=1, source_target_pairs={{0,12},{4,8},{8,4},{12,0},{1,13},{5,9},{9,5},{13,1},{2,14},{6,10},... | collective-permute-start | bytes 294920 | tf_op jit(solution)/shard_map/ppermute | solution.py:291
  17.7 5.9 %collective-permute-start.2 = (bf16[96,512]{1,0:T(8,128)(2,1)S(1)}, bf16[96,512]{1,0:T(8,128)(2,1)S(1)}, u32[]{:S(2)}, u32[]{:S(2)}) collective-permute-start(bf16[96,512]{1,0:T(8,128)(2,1)S(1)} %get-tuple-element.16.own_ref), channel_id=1, source_target_pairs={{0,12},{4,8},{8,4},{12,0},{1,13},{5,9},{9,5},{13,1},{2,14},{6,10},... | collective-permute-start | bytes 294920 | tf_op jit(solution)/shard_map/ppermute | solution.py:291
  55.7 19.3 %copy-start = (f32[32,256]{1,0:T(8,128)S(1)}, f32[32,256]{1,0:T(8,128)}, u32[]{:S(2)}) copy-start(f32[32,256]{1,0:T(8,128)} %d_ref.5) | copy-start | bytes 98308
  55.7 19.3 %copy-start.1 = (f32[32,256]{1,0:T(8,128)S(1)}, f32[32,256]{1,0:T(8,128)}, u32[]{:S(2)}) copy-start(f32[32,256]{1,0:T(8,128)} %r_ref.3) | copy-start | bytes 98308
  55.7 40.3 %copy-start.2 = (f32[32,256]{1,0:T(8,128)S(1)}, f32[32,256]{1,0:T(8,128)}, u32[]{:S(2)}) copy-start(f32[32,256]{1,0:T(8,128)} %coeffs_ref.1) | copy-start | bytes 98308
